TPU v7x, 512 devices: a whole 4x4x16 slice. The times are simulated.
512 devices in a mesh: fsdp: 16 (over z_hi, y), dp: 32 (over x, z_lo, core).
Axes of the slice: x: 4, y: 4, z: 16 (z_hi: 4, z_lo: 4; z = z_hi * 4 + z_lo), core: 2. Of those that a mesh axis runs over, the one named last changes fastest.
Arguments:
- noise_embed: bfloat16 [8192, 1024], P(('fsdp', 'dp')), may hold values from -6 to 6
- action_embed: bfloat16 [8192, 1024], P(('fsdp', 'dp')), may hold values from -6 to 6
- prefix_kv: bfloat16 [2, 512, 256, 256], P(None, ('fsdp', 'dp')), may hold values from -6 to 6
- flow_step: int32 [512], P(('fsdp', 'dp')), may hold values from 0 to 9
- action_mask: int32 [8192], P(('fsdp', 'dp')), may hold values 0 or 1
- w_up: bfloat16 [1024, 4096], P(None, 'fsdp'), may hold values from -0.1875 to 0.1875
- w_down: bfloat16 [4096, 1024], P('fsdp'), may hold values from -0.09375 to 0.09375
- query_grad: float32 [1024, 4096], P(None, 'fsdp'), may hold values from -6 to 6
Outputs:
- inverse_hvp: float32 [1024, 4096], P(None, 'fsdp')
- scores: float32 [512], P(('fsdp', 'dp'))
All inputs are finite; a program needn't handle non-finite values. No bound on the sum of `action_mask` on one device may be relied on, other than what follows from the above.
Results may differ from a plain program's by a relative error of at most 0.03.
Values may be sent and summed in bfloat16 or wider, within the bound.
No kernel may reach another device: no remote copies, remote signals or barrier semaphores. Data moves between devices by JAX's collectives and lax.ppermute only.
A program may use at most 64 MiB of HBM per device.

v0:
```python
import math

import jax
import jax.numpy as jnp
from jax import lax
from jax.sharding import PartitionSpec as P

D = 1024
FF = 4096
STEPS_T = 10
ITERS = 2


epsilon = 1e-06
sharpness_divisor = 6.0
damping_factor = 0.01


def attend(noise_embed, action_embed, prefix_kv, flow_step):
    demos = flow_step.shape[0]
    acts = noise_embed.shape[0] // demos
    channel_span = prefix_kv.shape[3]
    width = noise_embed.shape[1]
    times = (flow_step.astype(jnp.float32) + 1.0) / (STEPS_T + 1.0)
    per_token = jnp.repeat(times, acts)[:, None]
    noisy = noise_embed.astype(jnp.float32)
    clean = action_embed.astype(jnp.float32)
    inputs = per_token * noisy + (1.0 - per_token) * clean
    target = noisy - clean
    queries = inputs.reshape(demos, acts, width // channel_span, channel_span)
    probe_length = (
        queries * lax.rsqrt(jnp.mean(queries * queries, -1, keepdims=True) + epsilon)
    ).astype(jnp.bfloat16)
    keys = prefix_kv[0].astype(jnp.float32)
    lookup_length = (keys * lax.rsqrt(jnp.mean(keys * keys, -1, keepdims=True) + epsilon)).astype(
        jnp.bfloat16
    )
    match_energies = jnp.einsum(
        "zilf,zgf->zilg", probe_length, lookup_length, preferred_element_type=jnp.float32
    ) * (sharpness_divisor / channel_span)
    expo = jnp.exp(match_energies)
    weights = (expo / jnp.sum(expo, -1, keepdims=True)).astype(jnp.bfloat16)
    mixed = jnp.einsum("dahp,dpe->dahe", weights, prefix_kv[1], preferred_element_type=jnp.float32)
    hidden = inputs + mixed.reshape(demos * acts, width)
    normed_rows = (
        hidden * lax.rsqrt(jnp.mean(hidden * hidden, -1, keepdims=True) + epsilon)
    ).astype(jnp.bfloat16)
    return (hidden, normed_rows, target, acts)


def down_rows(source, w_down):
    return jnp.dot(source, w_down, preferred_element_type=jnp.float32)


def shards(noise_embed, action_embed, prefix_kv, flow_step, action_mask, w_up, w_down, query_grad):
    hidden, normed_rows, target, acts = attend(noise_embed, action_embed, prefix_kv, flow_step)
    tok_rows = normed_rows.shape[0]
    mask_own = action_mask.astype(jnp.float32)[:, None]
    gathered = lax.all_gather(normed_rows, "fsdp", axis=0, tiled=True)
    pre = jnp.dot(gathered, w_up, preferred_element_type=jnp.float32)
    sig = jax.nn.sigmoid(pre)
    slopes = sig * (1.0 + pre * (1.0 - sig))
    curves = sig * (1.0 - sig) * (2.0 + pre * (1.0 - 2.0 * sig))
    active = (pre * sig).astype(jnp.bfloat16)
    output = lax.psum_scatter(
        down_rows(active, w_down).astype(jnp.bfloat16), "fsdp", scatter_dimension=0, tiled=True
    ).astype(jnp.float32)
    err = (mask_own * (hidden + output - target)).astype(jnp.bfloat16)
    err_all, mask_all = (
        lax.all_gather(err, "fsdp", axis=0, tiled=True),
        lax.all_gather(action_mask.astype(jnp.bfloat16), "fsdp", axis=0, tiled=True),
    )
    pulled = jnp.dot(err_all, w_down.T, preferred_element_type=jnp.float32)
    back = pulled * slopes
    total = tok_rows * lax.axis_size("fsdp") * lax.axis_size("dp")
    vector = query_grad
    for step in range(ITERS):
        direction_vector = jnp.dot(
            gathered, vector.astype(jnp.bfloat16), preferred_element_type=jnp.float32
        )
        linear = (slopes * direction_vector).astype(jnp.bfloat16)
        moved = lax.psum_scatter(
            down_rows(linear, w_down).astype(jnp.bfloat16), "fsdp", scatter_dimension=0, tiled=True
        ).astype(jnp.float32)
        moved_err = (mask_own * moved).astype(jnp.bfloat16)
        moved_all = lax.all_gather(moved_err, "fsdp", axis=0, tiled=True)
        second = (
            jnp.dot(moved_all, w_down.T, preferred_element_type=jnp.float32) * slopes
            + pulled * curves * direction_vector
        ).astype(jnp.bfloat16)
        partial_hv = lax.dot_general(
            gathered, second, (((0,), (0,)), ((), ())), preferred_element_type=jnp.float32
        )
        aggregate_total = lax.psum(partial_hv.astype(jnp.bfloat16), "dp").astype(jnp.float32)
        vector = query_grad + (1.0 - damping_factor) * vector - aggregate_total / total
    projected = jnp.dot(gathered, vector.astype(jnp.bfloat16), preferred_element_type=jnp.float32)
    token_terms = jnp.sum(projected * back, -1)
    demo_terms = jnp.sum(token_terms.reshape(-1, acts), -1)
    owned = lax.psum_scatter(demo_terms, "fsdp", scatter_dimension=0, tiled=True)
    return (vector, -owned / (acts * math.sqrt(D * FF)))


def solution(mesh):
    placed = (
        P(("fsdp", "dp"), None),
        P(("fsdp", "dp"), None),
        P(None, ("fsdp", "dp"), None, None),
        P(("fsdp", "dp")),
        P(("fsdp", "dp")),
        P(None, "fsdp"),
        P("fsdp", None),
        P(None, "fsdp"),
    )
    return jax.shard_map(
        shards,
        mesh=mesh,
        in_specs=placed,
        out_specs=(P(None, "fsdp"), P(("fsdp", "dp"))),
        check_vma=False,
    )
```

profile of v0, /device:TPU:1, one launch (start us, length us, event | category | flops | bytes accessed | tf_op | source)
XLA Modules:
  0.0 1203.0 jit_solution(838447619523378574)
XLA Ops:
  7.9 0.8 fusion.36
  9.0 0.6 copy-done.4
  9.8 0.3 fusion.5
  10.1 0.2 convolution_bitcast_fusion
  10.5 57.2 %all_gather.12 = bf16[256,1024]{1,0:T(8,128)(2,1)S(1)} all-gather(bf16[16,1024]{1,0:T(8,128)(2,1)S(1)} %multiply_convert_fusion.8), channel_id=1, replica_groups=mesh['fsdp'=16,'dp'=32] {'fsdp'}, dimensions={0}, use_global_device_ids=true | all-gather | bytes 557056 | tf_op jit(solution)/shard_map/all_gather | solution.py:59
  67.7 0.3 fusion.12
  68.1 0.7 copy-done.6
  68.8 0.3 fusion.51
  69.1 1.2 convolution_convert_fusion.4
  70.4 1.1 convolution_convert_fusion.3
  71.6 0.6 copy-done.8
  72.2 109.2 %reduce-scatter.4.cloned.1.call-done = bf16[16,1024]{1,0:T(8,128)(2,1)} async-done(((bf16[256,1024]{1,0:T(8,128)(2,1)}), bf16[16,1024]{1,0:T(8,128)(2,1)}) %reduce-scatter.4.cloned.1.call-update) | async-done | bytes 32784 | tf_op jit(solution)/shard_map/reduce_scatter | solution.py:82
  181.4 111.9 %reduce-scatter.6.cloned.1.call-done = bf16[16,1024]{1,0:T(8,128)(2,1)} async-done(((bf16[256,1024]{1,0:T(8,128)(2,1)}), bf16[16,1024]{1,0:T(8,128)(2,1)}) %reduce-scatter.6.cloned.1.call-update) | async-done | bytes 32784 | tf_op jit(solution)/shard_map/reduce_scatter | solution.py:65
  293.3 0.9 fusion.34
  294.2 50.2 %all_gather.14 = bf16[256,1024]{1,0:T(8,128)(2,1)S(1)} all-gather(bf16[16,1024]{1,0:T(8,128)(2,1)S(1)} %get-tuple-element.2), channel_id=1, replica_groups=mesh['fsdp'=16,'dp'=32] {'fsdp'}, dimensions={0}, use_global_device_ids=true | all-gather | bytes 557056 | tf_op jit(solution)/shard_map/all_gather | solution.py:70
  344.4 0.3 fusion.52
  344.8 44.9 %all_gather.13 = bf16[256,1024]{1,0:T(8,128)(2,1)S(1)} all-gather(bf16[16,1024]{1,0:T(8,128)(2,1)S(1)} %get-tuple-element.3), channel_id=1, replica_groups=mesh['fsdp'=16,'dp'=32] {'fsdp'}, dimensions={0}, use_global_device_ids=true | all-gather | bytes 557056 | tf_op jit(solution)/shard_map/all_gather | solution.py:86
  389.7 1.7 convolution_convert_fusion.2
  391.4 298.2 %all-reduce.4.cloned.1.call-done = bf16[1024,256]{1,0:T(8,128)(2,1)} async-done(((bf16[1024,256]{1,0:T(8,128)(2,1)}), bf16[1024,256]{1,0:T(8,128)(2,1)}) %all-reduce.4.cloned.1.call-update) | async-done | bytes 524304 | tf_op jit(solution)/shard_map/psum | solution.py:94
  689.6 1.4 fusion.8
  691.1 1.2 convolution_convert_fusion.1
  692.3 111.5 %reduce-scatter.8.cloned.1.call-done = bf16[16,1024]{1,0:T(8,128)(2,1)} async-done(((bf16[256,1024]{1,0:T(8,128)(2,1)}), bf16[16,1024]{1,0:T(8,128)(2,1)}) %reduce-scatter.8.cloned.1.call-update) | async-done | bytes 32784 | tf_op jit(solution)/shard_map/reduce_scatter | solution.py:82
  803.8 0.8 multiply_convert_fusion.6
  804.6 49.9 %all_gather.15 = bf16[256,1024]{1,0:T(8,128)(2,1)S(1)} all-gather(bf16[16,1024]{1,0:T(8,128)(2,1)S(1)} %multiply_convert_fusion.6), channel_id=1, replica_groups=mesh['fsdp'=16,'dp'=32] {'fsdp'}, dimensions={0}, use_global_device_ids=true | all-gather | bytes 557056 | tf_op jit(solution)/shard_map/all_gather | solution.py:86
  854.5 1.7 convolution_convert_fusion
  856.2 1.3 dynamic-slice
  857.5 287.9 %all-reduce.6.cloned.1.call-done = bf16[1024,256]{1,0:T(8,128)(2,1)} async-done(((bf16[1024,256]{1,0:T(8,128)(2,1)}), bf16[1024,256]{1,0:T(8,128)(2,1)}) %all-reduce.6.cloned.1.call-update) | async-done | bytes 524304 | tf_op jit(solution)/shard_map/psum | solution.py:94
  1145.4 1.4 multiply_subtract_fusion
  1146.8 1.0 copy-done.3
  1147.8 0.4 fusion.4
  1148.4 45.0 %all-reduce = f32[16]{0:T(128)S(1)} all-reduce(f32[16]{0:T(128)S(1)} %reduce_sum.59), channel_id=5, replica_groups=mesh['fsdp'=16,'dp'=32] {'fsdp'}, use_global_device_ids=true, to_apply=%region_11.0.clone | all-reduce | flops 16 | bytes 128
  1193.4 1.3 dynamic-slice.1
  (39 shorter events, 1.1 us)
Async XLA Ops:
  7.2 62.0 %copy-start = (bf16[256,1024]{1,0:T(8,128)(2,1)S(1)}, bf16[256,1024]{1,0:T(8,128)(2,1)}, u32[]{:S(2)}) copy-start(bf16[256,1024]{1,0:T(8,128)(2,1)} %param.14) | copy-start | bytes 1572868
  7.2 174.3 %reduce-scatter.4.cloned.1.call-start = ((), (), s32[]{:S(2)}) async-start(), calls=%async_computation.3 | async-start | bytes 557056 | tf_op jit(solution)/shard_map/reduce_scatter | solution.py:82
  8.7 1.0 copy-start.7
  8.9 0.8 copy-start.4
  8.9 0.8 copy-start.5
  9.0 58.7 %copy-start.1 = (f32[1024,256]{1,0:T(8,128)S(1)}, f32[1024,256]{1,0:T(8,128)}, u32[]{:S(2)}) copy-start(f32[1024,256]{1,0:T(8,128)} %param.15) | copy-start | bytes 3145732
  67.7 1.0 copy-start.6
  70.3 223.0 %reduce-scatter.6.cloned.1.call-start = ((), (), s32[]{:S(2)}) async-start(), calls=%async_computation.4 | async-start | bytes 557056 | tf_op jit(solution)/shard_map/reduce_scatter | solution.py:65
  71.5 0.7 copy-start.8
  71.6 618.1 %all-reduce.4.cloned.1.call-start = ((), (), s32[]{:S(2)}) async-start(), calls=%async_computation.5 | async-start | bytes 1048576 | tf_op jit(solution)/shard_map/psum | solution.py:94
  391.4 412.4 %reduce-scatter.8.cloned.1.call-start = ((), (), s32[]{:S(2)}) async-start(), calls=%async_computation.6 | async-start | bytes 557056 | tf_op jit(solution)/shard_map/reduce_scatter | solution.py:82
  692.3 453.1 %all-reduce.6.cloned.1.call-start = ((), (), s32[]{:S(2)}) async-start(), calls=%async_computation.7 | async-start | bytes 1048576 | tf_op jit(solution)/shard_map/psum | solution.py:94
  856.2 289.3 %copy-start.2 = (bf16[1024,256]{1,0:T(8,128)(2,1)S(1)}, bf16[1024,256]{1,0:T(8,128)(2,1)}, u32[]{:S(2)}) copy-start(bf16[1024,256]{1,0:T(8,128)(2,1)} %all-reduce.4.cloned.1.call-done) | copy-start | bytes 1572868
  1146.8 1.0 copy-start.3
Sparse Core Ops, SparseCore 0:
  70.4 110.9 reduce-scatter.3
  186.6 106.6 reduce-scatter.5
  391.5 298.1 all-reduce.3
  694.7 109.0 reduce-scatter.7
  856.3 289.0 all-reduce.5
where the time goes:
time: 1210 us; the launch traced here: 1200 us
  waiting for transfers between devices  919 us (76%)
  blocking collectives  247 us (20%)
  between operations  16.5 us (1%)
    psum x2, waiting for transfers between devices, shards(): lax.psum(partial_hv.astype(jnp.bfloat16), 'dp').astype(jnp.float32)  586 us
    reduce_scatter x2, waiting for transfers between devices, shards(): lax.psum_scatter(down_rows(linear, w_down).astype(jnp.bfloat16), 'fsdp',...  221 us
    reduce_scatter x1, waiting for transfers between devices, shards(): lax.psum_scatter(down_rows(active, w_down).astype(jnp.bfloat16), 'fsdp',...  112 us
    all_gather x2, blocking collectives, shards(): moved_all = lax.all_gather(moved_err, 'fsdp', axis=0, tiled=True)  94.7 us
    all_gather x1, blocking collectives, shards(): gathered = lax.all_gather(normed_rows, 'fsdp', axis=0, tiled=True)  57.2 us
    all_gather x1, blocking collectives, shards(): lax.all_gather(err, 'fsdp', axis=0, tiled=True)  50.2 us
    unnamed x1, blocking collectives  45 us
  transfers between devices with their start and end apart: 5, of which 5 were waited for; matrix products, arithmetic and copies ran while one was open for 0% of the time, Pallas kernels for 0%

commit v1 on v0

v1 whole, which is shorter than its diff:
```python
import math

import jax
import jax.numpy as jnp
from jax import lax
from jax.sharding import Mesh
from jax.sharding import PartitionSpec as P

D = 1024
FF = 4096
STEPS_T = 10
ITERS = 2

epsilon = 1e-06
sharpness_divisor = 6.0
damping_factor = 0.01

AXES = ("zh", "y", "x", "zl", "c")
SIZES = (4, 4, 4, 4, 2)
GRID = ("x", "zl")


def attend(noise_embed, action_embed, prefix_kv, flow_step):
    demos = flow_step.shape[0]
    acts = noise_embed.shape[0] // demos
    channel_span = prefix_kv.shape[3]
    width = noise_embed.shape[1]
    times = (flow_step.astype(jnp.float32) + 1.0) / (STEPS_T + 1.0)
    per_token = jnp.repeat(times, acts)[:, None]
    noisy = noise_embed.astype(jnp.float32)
    clean = action_embed.astype(jnp.float32)
    inputs = per_token * noisy + (1.0 - per_token) * clean
    target = noisy - clean
    queries = inputs.reshape(demos, acts, width // channel_span, channel_span)
    probe_length = (
        queries * lax.rsqrt(jnp.mean(queries * queries, -1, keepdims=True) + epsilon)
    ).astype(jnp.bfloat16)
    keys = prefix_kv[0].astype(jnp.float32)
    lookup_length = (keys * lax.rsqrt(jnp.mean(keys * keys, -1, keepdims=True) + epsilon)).astype(
        jnp.bfloat16
    )
    match_energies = jnp.einsum(
        "zilf,zgf->zilg", probe_length, lookup_length, preferred_element_type=jnp.float32
    ) * (sharpness_divisor / channel_span)
    expo = jnp.exp(match_energies)
    weights = (expo / jnp.sum(expo, -1, keepdims=True)).astype(jnp.bfloat16)
    mixed = jnp.einsum("dahp,dpe->dahe", weights, prefix_kv[1], preferred_element_type=jnp.float32)
    hidden = inputs + mixed.reshape(demos * acts, width)
    normed_rows = (
        hidden * lax.rsqrt(jnp.mean(hidden * hidden, -1, keepdims=True) + epsilon)
    ).astype(jnp.bfloat16)
    return (hidden, normed_rows, target, acts)


def swap(blocks, axes):
    return lax.all_to_all(blocks, axes, 0, 0)


def collect(block, axes, members):
    return swap(jnp.broadcast_to(block[None], (members, *block.shape)), axes)


def total(blocks):
    return jnp.sum(blocks.astype(jnp.float32), 0)


def scatter_tokens(parts):
    parts = parts.astype(jnp.bfloat16)
    parts = parts.reshape(4, 4, *parts.shape[1:])
    stage = total(swap(jnp.swapaxes(parts, 0, 1), "y")).astype(jnp.bfloat16)
    return total(swap(stage, "zh"))


def gather_tokens(block):
    stage = collect(block, "zh", 4)
    full = jnp.swapaxes(collect(stage, "y", 4), 0, 1)
    return full.reshape(16, *block.shape)


def sum_copies(part):
    columns = part.shape[1]
    half = D // 2
    pair = total(swap(part.astype(jnp.bfloat16).reshape(2, half, columns), "c"))
    rows = total(swap(pair.astype(jnp.bfloat16).reshape(16, half // 16, columns), GRID))
    rows = collect(rows.astype(jnp.bfloat16), GRID, 16).reshape(half, columns)
    return collect(rows, "c", 2).reshape(D, columns)


def shards(noise_embed, action_embed, prefix_kv, flow_step, action_mask, w_up, w_down, query_grad):
    hidden, normed_rows, target, acts = attend(noise_embed, action_embed, prefix_kv, flow_step)
    tok_rows = normed_rows.shape[0]
    members = 16
    tokens = tok_rows * members
    mask_own = action_mask.astype(jnp.float32)[:, None]
    gathered = gather_tokens(normed_rows).reshape(tokens, D)

    def down(source):
        return jnp.dot(source, w_down, preferred_element_type=jnp.float32)

    def up(source):
        return jnp.dot(source, w_down.T, preferred_element_type=jnp.float32)

    def project(vector):
        return jnp.dot(gathered, vector.astype(jnp.bfloat16), preferred_element_type=jnp.float32)

    pre = jnp.dot(gathered, w_up, preferred_element_type=jnp.float32)
    sig = jax.nn.sigmoid(pre)
    slopes = sig * (1.0 + pre * (1.0 - sig))
    curves = sig * (1.0 - sig) * (2.0 + pre * (1.0 - 2.0 * sig))
    active = (pre * sig).astype(jnp.bfloat16)
    count = tokens * 32

    vector = query_grad
    pulled = None
    for step in range(ITERS):
        tangent = project(vector)
        linear = (slopes * tangent).astype(jnp.bfloat16)
        moved_part = down(linear).astype(jnp.bfloat16).reshape(members, tok_rows, D)
        if step == 0:
            out_part = down(active).astype(jnp.bfloat16).reshape(members, tok_rows, D)
            both = scatter_tokens(jnp.stack([out_part, moved_part], 1))
            err = (mask_own * (hidden + both[0] - target)).astype(jnp.bfloat16)
            moved_err = (mask_own * both[1]).astype(jnp.bfloat16)
            both = gather_tokens(jnp.stack([err, moved_err], 0))
            pulled = up(both[:, 0].reshape(tokens, D))
            moved_all = both[:, 1].reshape(tokens, D)
        else:
            moved = scatter_tokens(moved_part)
            moved_all = gather_tokens((mask_own * moved).astype(jnp.bfloat16)).reshape(tokens, D)
        second = (up(moved_all) * slopes + pulled * curves * tangent).astype(jnp.bfloat16)
        part = lax.dot_general(
            gathered, second, (((0,), (0,)), ((), ())), preferred_element_type=jnp.float32
        )
        product = sum_copies(part).astype(jnp.float32)
        vector = query_grad + (1.0 - damping_factor) * vector - product / count
    back = pulled * slopes
    token_terms = jnp.sum(project(vector) * back, -1)
    demo_terms = jnp.sum(token_terms.reshape(-1, acts), -1)
    owned = jnp.sum(swap(demo_terms.reshape(members, -1), ("zh", "y")), 0)
    return (vector, -owned / (acts * math.sqrt(D * FF)))


def solution(mesh):
    fine = Mesh(mesh.devices.reshape(SIZES), AXES)
    fsdp, everyone = AXES[:2], AXES
    placed = (
        P(everyone, None),
        P(everyone, None),
        P(None, everyone, None, None),
        P(everyone),
        P(everyone),
        P(None, fsdp),
        P(fsdp, None),
        P(None, fsdp),
    )
    return jax.shard_map(
        shards,
        mesh=fine,
        in_specs=placed,
        out_specs=(P(None, fsdp), P(everyone)),
        check_vma=False,
    )
```

time: 1210 us -> 296 us (0.24)
  waiting for transfers between devices: 919 us -> 12.9 us
  between operations: 16.5 us -> 3.56 us
    psum x2 -> x0, waiting for transfers between devices: 586 us -> none  [shards(): lax.psum(partial_hv.astype(jnp.bfloat16), 'dp').astype(jnp.float32)]
    reduce_scatter x3 -> x0, waiting for transfers between devices: 333 us -> none  [the longest x2 221 us: shards(): lax.psum_scatter(down_rows(linear, w_down).astype(jnp.bfloat16), 'fsdp',...]
    all_to_all x0 -> x18, blocking collectives: none -> 250 us  [swap(): return lax.all_to_all(blocks, axes, 0, 0)]
    all_gather x4 -> x0, blocking collectives: 202 us -> none  [the longest x2 94.7 us: shards(): moved_all = lax.all_gather(moved_err, 'fsdp', axis=0, tiled=True)]
    unnamed x1 -> x0, blocking collectives: 45 us -> none
    all_to_all x0 -> x1, waiting for transfers between devices: none -> 12.9 us  [swap(): return lax.all_to_all(blocks, axes, 0, 0)]
  transfers between devices with their start and end apart: 5 -> 1, of which waited for: 5 -> 1; matrix products, arithmetic and copies ran while one was open for 0% -> 0% of each run, Pallas kernels for 0% -> 0%
where the time goes in v1:
time: 296 us; the launch traced here: 294 us
  blocking collectives  250 us (84%)
  waiting for transfers between devices  12.9 us (4%)
  matrix products  8.79 us (3%)
  other arithmetic  6.55 us (2%)
  starting transfers between devices  6.35 us (2%)
  local copies, waits for them, and re-layouts  6.26 us (2%)
  between operations  3.56 us (1%)
    all_to_all x18, blocking collectives, swap(): return lax.all_to_all(blocks, axes, 0, 0)  250 us
    all_to_all x1, waiting for transfers between devices, swap(): return lax.all_to_all(blocks, axes, 0, 0)  12.9 us
    all_to_all x1, starting transfers between devices, swap(): return lax.all_to_all(blocks, axes, 0, 0)  6.35 us
  transfers between devices with their start and end apart: 1, of which 1 were waited for; matrix products, arithmetic and copies ran while one was open for 0% of the time, Pallas kernels for 0%

profile of v1, /device:TPU:1, one launch (start us, length us, event | category | flops | bytes accessed | tf_op | source)
XLA Modules:
  0.0 294.4 jit_solution(8594285361350973526)
XLA Ops:
  1.4 1.0 fusion.14
  2.8 0.7 copy-done.13
  4.2 28.1 %all_to_all.99 = bf16[4,16,1024]{2,1,0:T(8,128)(2,1)S(1)} all-to-all(bf16[4,16,1024]{2,1,0:T(8,128)(2,1)S(1)} %broadcast_in_dim.24), channel_id=1, replica_groups=mesh['zh'=4,'y'=4,'x'=4,'zl'=4,'c'=2] {'zh'}, dimensions={0} | all-to-all | bytes 262144 | tf_op jit(solution)/shard_map/all_to_all | solution.py:56
  32.4 11.0 %all_to_all.100 = bf16[4,4,16,1024]{3,2,1,0:T(8,128)(2,1)S(1)} all-to-all(bf16[4,4,16,1024]{3,2,1,0:T(8,128)(2,1)S(1)} %broadcast_in_dim.25), channel_id=1, replica_groups=mesh['zh'=4,'y'=4,'x'=4,'zl'=4,'c'=2] {'y'}, dimensions={0} | all-to-all | bytes 1048576 | tf_op jit(solution)/shard_map/all_to_all | solution.py:56
  43.8 0.8 copy-done.1
  46.2 13.1 %all_to_all.101 = bf16[4,4,2,16,1024]{4,3,1,2,0:T(8,128)(2,1)S(1)} all-to-all(bf16[4,4,2,16,1024]{4,3,1,2,0:T(8,128)(2,1)S(1)} %copy_bitcast_fusion), channel_id=1, replica_groups=mesh['zh'=4,'y'=4,'x'=4,'zl'=4,'c'=2] {'y'}, dimensions={0} | all-to-all | bytes 2097152 | tf_op jit(solution)/shard_map/all_to_all | solution.py:56
  59.5 0.7 copy.61
  60.2 6.4 %all-to-all-start.3 = ((bf16[4,2,16,1024]{3,2,1,0:T(8,128)(2,1)}), bf16[4,2,16,1024]{3,2,1,0:T(8,128)(2,1)S(1)}, u32[]{:S(2)}, u32[]{:S(2)}) async-start(bf16[4,2,16,1024]{3,2,1,0:T(8,128)(2,1)} %copy.61), calls=%async_computation.3 | async-start | bytes 524288 | tf_op jit(solution)/shard_map/all_to_all | solution.py:56
  66.6 12.9 %all-to-all-done.3 = bf16[4,2,16,1024]{3,2,1,0:T(8,128)(2,1)S(1)} async-done(((bf16[4,2,16,1024]{3,2,1,0:T(8,128)(2,1)}), bf16[4,2,16,1024]{3,2,1,0:T(8,128)(2,1)S(1)}, u32[]{:S(2)}, u32[]{:S(2)}) %all-to-all-start.3) | async-done | bytes 262176 | tf_op jit(solution)/shard_map/all_to_all | solution.py:56
  79.7 15.5 %all_to_all.102 = bf16[4,2,16,1024]{3,2,1,0:T(8,128)(2,1)S(1)} all-to-all(bf16[4,2,16,1024]{3,2,1,0:T(8,128)(2,1)S(1)} %broadcast_in_dim.26), channel_id=1, replica_groups=mesh['zh'=4,'y'=4,'x'=4,'zl'=4,'c'=2] {'zh'}, dimensions={0} | all-to-all | bytes 524288 | tf_op jit(solution)/shard_map/all_to_all | solution.py:56
  95.3 12.5 %all_to_all.103 = bf16[4,4,2,16,1024]{4,3,2,1,0:T(8,128)(2,1)S(1)} all-to-all(bf16[4,4,2,16,1024]{4,3,2,1,0:T(8,128)(2,1)S(1)} %broadcast_in_dim.27), channel_id=1, replica_groups=mesh['zh'=4,'y'=4,'x'=4,'zl'=4,'c'=2] {'y'}, dimensions={0} | all-to-all | bytes 2097152 | tf_op jit(solution)/shard_map/all_to_all | solution.py:56
  108.0 1.1 fusion.51
  109.1 1.9 convolution_convert_fusion.2
  111.0 20.2 %all_to_all.104 = bf16[2,512,256]{2,1,0:T(8,128)(2,1)S(1)} all-to-all(bf16[2,512,256]{2,1,0:T(8,128)(2,1)S(1)} %bitcast.106), channel_id=1, replica_groups=mesh['zh'=4,'y'=4,'x'=4,'zl'=4,'c'=2] {'c'}, dimensions={0} | all-to-all | bytes 1048576 | tf_op jit(solution)/shard_map/all_to_all | solution.py:56
  131.4 16.8 %all_to_all.105 = bf16[16,32,256]{2,1,0:T(8,128)(2,1)S(1)} all-to-all(bf16[16,32,256]{2,1,0:T(8,128)(2,1)S(1)} %bitcast.104), channel_id=1, replica_groups=mesh['zh'=4,'y'=4,'x'=4,'zl'=4,'c'=2] {'x','zl'}, dimensions={0} | all-to-all | bytes 524288 | tf_op jit(solution)/shard_map/all_to_all | solution.py:56
  148.3 13.1 %all_to_all.106 = bf16[16,32,256]{2,1,0:T(8,128)(2,1)S(1)} all-to-all(bf16[16,32,256]{2,1,0:T(8,128)(2,1)S(1)} %broadcast_in_dim.28), channel_id=1, replica_groups=mesh['zh'=4,'y'=4,'x'=4,'zl'=4,'c'=2] {'x','zl'}, dimensions={0} | all-to-all | bytes 524288 | tf_op jit(solution)/shard_map/all_to_all | solution.py:56
  161.5 6.0 %all_to_all.107 = bf16[2,512,256]{2,1,0:T(8,128)(2,1)S(1)} all-to-all(bf16[2,512,256]{2,1,0:T(8,128)(2,1)S(1)} %broadcast_in_dim.30), channel_id=1, replica_groups=mesh['zh'=4,'y'=4,'x'=4,'zl'=4,'c'=2] {'c'}, dimensions={0} | all-to-all | bytes 1048576 | tf_op jit(solution)/shard_map/all_to_all | solution.py:56
  169.4 12.3 %all_to_all.108 = bf16[4,4,16,1024]{3,2,1,0:T(8,128)(2,1)} all-to-all(bf16[4,4,16,1024]{3,2,1,0:T(8,128)(2,1)S(1)} %bitcast.97), channel_id=1, replica_groups=mesh['zh'=4,'y'=4,'x'=4,'zl'=4,'c'=2] {'y'}, dimensions={0} | all-to-all | bytes 1048576 | tf_op jit(solution)/shard_map/all_to_all | solution.py:56
  181.8 1.1 reduce_sum.161
  182.9 15.3 %all_to_all.109 = bf16[4,16,1024]{2,1,0:T(8,128)(2,1)S(1)} all-to-all(bf16[4,16,1024]{2,1,0:T(8,128)(2,1)S(1)} %reduce_sum.161), channel_id=1, replica_groups=mesh['zh'=4,'y'=4,'x'=4,'zl'=4,'c'=2] {'zh'}, dimensions={0} | all-to-all | bytes 262144 | tf_op jit(solution)/shard_map/all_to_all | solution.py:56
  198.3 16.9 %all_to_all.110 = bf16[4,16,1024]{2,1,0:T(8,128)(2,1)S(1)} all-to-all(bf16[4,16,1024]{2,1,0:T(8,128)(2,1)S(1)} %broadcast_in_dim.31), channel_id=1, replica_groups=mesh['zh'=4,'y'=4,'x'=4,'zl'=4,'c'=2] {'zh'}, dimensions={0} | all-to-all | bytes 262144 | tf_op jit(solution)/shard_map/all_to_all | solution.py:56
  215.2 9.4 %all_to_all.111 = bf16[4,4,16,1024]{3,2,1,0:T(8,128)(2,1)S(1)} all-to-all(bf16[4,4,16,1024]{3,2,1,0:T(8,128)(2,1)S(1)} %broadcast_in_dim.32), channel_id=1, replica_groups=mesh['zh'=4,'y'=4,'x'=4,'zl'=4,'c'=2] {'y'}, dimensions={0} | all-to-all | bytes 1048576 | tf_op jit(solution)/shard_map/all_to_all | solution.py:56
  224.6 0.8 copy.67
  225.4 2.9 convolution_convert_fusion
  228.3 10.0 %all_to_all.112 = bf16[2,512,256]{2,1,0:T(8,128)(2,1)} all-to-all(bf16[2,512,256]{2,1,0:T(8,128)(2,1)} %bitcast.108), channel_id=1, replica_groups=mesh['zh'=4,'y'=4,'x'=4,'zl'=4,'c'=2] {'c'}, dimensions={0} | all-to-all | bytes 1048576 | tf_op jit(solution)/shard_map/all_to_all | solution.py:56
  238.3 1.9 reduce_sum.163
  240.2 14.4 %all_to_all.113 = bf16[16,32,256]{2,1,0:T(8,128)(2,1)S(1)} all-to-all(bf16[16,32,256]{2,1,0:T(8,128)(2,1)} %bitcast.105), channel_id=1, replica_groups=mesh['zh'=4,'y'=4,'x'=4,'zl'=4,'c'=2] {'x','zl'}, dimensions={0} | all-to-all | bytes 524288 | tf_op jit(solution)/shard_map/all_to_all | solution.py:56
  254.6 13.1 %all_to_all.114 = bf16[16,32,256]{2,1,0:T(8,128)(2,1)S(1)} all-to-all(bf16[16,32,256]{2,1,0:T(8,128)(2,1)S(1)} %broadcast_in_dim.33), channel_id=1, replica_groups=mesh['zh'=4,'y'=4,'x'=4,'zl'=4,'c'=2] {'x','zl'}, dimensions={0} | all-to-all | bytes 524288 | tf_op jit(solution)/shard_map/all_to_all | solution.py:56
  267.8 6.0 %all_to_all.115 = bf16[2,512,256]{2,1,0:T(8,128)(2,1)S(1)} all-to-all(bf16[2,512,256]{2,1,0:T(8,128)(2,1)S(1)} %broadcast_in_dim.35), channel_id=1, replica_groups=mesh['zh'=4,'y'=4,'x'=4,'zl'=4,'c'=2] {'c'}, dimensions={0} | all-to-all | bytes 1048576 | tf_op jit(solution)/shard_map/all_to_all | solution.py:56
  274.2 1.0 copy-done.2
  275.8 16.2 %all_to_all.116 = f32[16,1,1]{2,1,0:T(1,128)S(1)} all-to-all(f32[16,1,1]{2,1,0:T(1,128)S(1)} %copy.70), channel_id=1, replica_groups=mesh['zh'=4,'y'=4,'x'=4,'zl'=4,'c'=2] {'zh','y'}, dimensions={0} | all-to-all | bytes 128 | tf_op jit(solution)/shard_map/all_to_all | solution.py:56
  292.0 0.6 reduce_sum.167
  (81 shorter events, 7.1 us)
Async XLA Ops:
  0.6 44.4 %copy-start = (bf16[256,1024]{1,0:T(8,128)(2,1)S(1)}, bf16[256,1024]{1,0:T(8,128)(2,1)}, u32[]{:S(2)}) copy-start(bf16[256,1024]{1,0:T(8,128)(2,1)} %param.14) | copy-start | bytes 1572868
  1.3 1.1 copy-start.3
  1.4 1.1 copy-start.4
  2.5 1.0 copy-start.13
  32.3 11.1 %copy-start.5 = (bf16[1024,256]{1,0:T(8,128)(2,1)S(1)}, bf16[1024,256]{1,0:T(8,128)(2,1)}, u32[]{:S(2)}) copy-start(bf16[1024,256]{1,0:T(8,128)(2,1)} %param.13) | copy-start | bytes 1572868
  43.4 1.2 copy-start.1
  44.6 0.7 copy-start.6
  45.0 0.7 copy-start.11
  60.2 6.4 %copy-start.14 = (s32[16]{0:T(128)S(1)}, s32[16]{0:T(128)}, u32[]{:S(2)}) copy-start(s32[16]{0:T(128)} %param.12) | copy-start | bytes 196
  60.2 19.3 %all-to-all-start.3 = ((bf16[4,2,16,1024]{3,2,1,0:T(8,128)(2,1)}), bf16[4,2,16,1024]{3,2,1,0:T(8,128)(2,1)S(1)}, u32[]{:S(2)}, u32[]{:S(2)}) async-start(bf16[4,2,16,1024]{3,2,1,0:T(8,128)(2,1)} %copy.61), calls=%async_computation.3 | async-start | bytes 524288 | tf_op jit(solution)/shard_map/all_to_all | solution.py:56
  108.0 1.1 copy-start.7
  167.7 1.0 copy-start.8
  168.7 0.7 copy-start.12
  273.9 1.2 copy-start.9
  273.9 1.2 copy-start.10
  274.2 1.0 copy-start.2

commit v2 on v1

--- a/solution.py
+++ b/solution.py
@@ -9,7 +9,6 @@
 D = 1024
 FF = 4096
 STEPS_T = 10
-ITERS = 2
 
 epsilon = 1e-06
 sharpness_divisor = 6.0
@@ -64,38 +63,26 @@
     return jnp.sum(blocks.astype(jnp.float32), 0)
 
 
-def scatter_tokens(parts):
-    parts = parts.astype(jnp.bfloat16)
-    parts = parts.reshape(4, 4, *parts.shape[1:])
-    stage = total(swap(jnp.swapaxes(parts, 0, 1), "y")).astype(jnp.bfloat16)
-    return total(swap(stage, "zh"))
-
-
-def gather_tokens(block):
-    stage = collect(block, "zh", 4)
-    full = jnp.swapaxes(collect(stage, "y", 4), 0, 1)
-    return full.reshape(16, *block.shape)
-
-
 def sum_copies(part):
     columns = part.shape[1]
     half = D // 2
     pair = total(swap(part.astype(jnp.bfloat16).reshape(2, half, columns), "c"))
     rows = total(swap(pair.astype(jnp.bfloat16).reshape(16, half // 16, columns), GRID))
     rows = collect(rows.astype(jnp.bfloat16), GRID, 16).reshape(half, columns)
-    return collect(rows, "c", 2).reshape(D, columns)
+    return lax.all_gather(rows, "c", axis=0, tiled=True)
 
 
 def shards(noise_embed, action_embed, prefix_kv, flow_step, action_mask, w_up, w_down, query_grad):
     hidden, normed_rows, target, acts = attend(noise_embed, action_embed, prefix_kv, flow_step)
-    tok_rows = normed_rows.shape[0]
-    members = 16
-    tokens = tok_rows * members
+    own = normed_rows.shape[0]
+    tokens = own * 16
+    count = tokens * 32
     mask_own = action_mask.astype(jnp.float32)[:, None]
-    gathered = gather_tokens(normed_rows).reshape(tokens, D)
+    sent = normed_rows * action_mask.astype(jnp.bfloat16)[:, None]
+    gathered = collect(collect(sent, "zh", 4), "y", 4).reshape(tokens, D)
 
     def down(source):
-        return jnp.dot(source, w_down, preferred_element_type=jnp.float32)
+        return jnp.dot(source, w_down, preferred_element_type=jnp.float32).astype(jnp.bfloat16)
 
     def up(source):
         return jnp.dot(source, w_down.T, preferred_element_type=jnp.float32)
@@ -103,40 +90,45 @@
     def project(vector):
         return jnp.dot(gathered, vector.astype(jnp.bfloat16), preferred_element_type=jnp.float32)
 
+    def hvp(second):
+        part = lax.dot_general(
+            gathered, second, (((0,), (0,)), ((), ())), preferred_element_type=jnp.float32
+        )
+        return sum_copies(part).astype(jnp.float32) / count
+
+    units = w_up.shape[1]
     pre = jnp.dot(gathered, w_up, preferred_element_type=jnp.float32)
     sig = jax.nn.sigmoid(pre)
     slopes = sig * (1.0 + pre * (1.0 - sig))
     curves = sig * (1.0 - sig) * (2.0 + pre * (1.0 - 2.0 * sig))
     active = (pre * sig).astype(jnp.bfloat16)
-    count = tokens * 32
+    tangent = project(query_grad)
+    linear = (slopes * tangent).astype(jnp.bfloat16)
+    source = jnp.stack([active.reshape(16, own, units), linear.reshape(16, own, units)], 1)
+    parts = down(source.reshape(2 * tokens, units)).reshape(4, 4, 2, own, D)
+    stage = total(swap(parts, "y")).astype(jnp.bfloat16)
+    both = total(swap(stage, "zh"))
+    err = (mask_own * (hidden + both[0] - target)).astype(jnp.bfloat16)
+    moved_err = (mask_own * both[1]).astype(jnp.bfloat16)
+    both = lax.all_gather(jnp.stack([err, moved_err], 0), "zh", axis=0)
+    both = up(collect(both, "y", 4).reshape(2 * tokens, D)).reshape(16, 2, own, units)
+    pulled = both[:, 0].reshape(tokens, units)
+    moved = both[:, 1].reshape(tokens, units)
+    bend = pulled * curves
+    vector = query_grad + (1.0 - damping_factor) * query_grad
+    vector = vector - hvp((moved * slopes + bend * tangent).astype(jnp.bfloat16))
 
-    vector = query_grad
-    pulled = None
-    for step in range(ITERS):
-        tangent = project(vector)
-        linear = (slopes * tangent).astype(jnp.bfloat16)
-        moved_part = down(linear).astype(jnp.bfloat16).reshape(members, tok_rows, D)
-        if step == 0:
-            out_part = down(active).astype(jnp.bfloat16).reshape(members, tok_rows, D)
-            both = scatter_tokens(jnp.stack([out_part, moved_part], 1))
-            err = (mask_own * (hidden + both[0] - target)).astype(jnp.bfloat16)
-            moved_err = (mask_own * both[1]).astype(jnp.bfloat16)
-            both = gather_tokens(jnp.stack([err, moved_err], 0))
-            pulled = up(both[:, 0].reshape(tokens, D))
-            moved_all = both[:, 1].reshape(tokens, D)
-        else:
-            moved = scatter_tokens(moved_part)
-            moved_all = gather_tokens((mask_own * moved).astype(jnp.bfloat16)).reshape(tokens, D)
-        second = (up(moved_all) * slopes + pulled * curves * tangent).astype(jnp.bfloat16)
-        part = lax.dot_general(
-            gathered, second, (((0,), (0,)), ((), ())), preferred_element_type=jnp.float32
-        )
-        product = sum_copies(part).astype(jnp.float32)
-        vector = query_grad + (1.0 - damping_factor) * vector - product / count
-    back = pulled * slopes
-    token_terms = jnp.sum(project(vector) * back, -1)
+    tangent = project(vector)
+    parts = down((slopes * tangent).astype(jnp.bfloat16)).reshape(4, 4 * own, D)
+    stage = total(swap(parts, "y")).astype(jnp.bfloat16)
+    stage = total(lax.all_gather(stage, "zh", axis=0)).astype(jnp.bfloat16)
+    moved = up(collect(stage, "y", 4).reshape(tokens, D))
+    vector = query_grad + (1.0 - damping_factor) * vector
+    vector = vector - hvp((moved * slopes + bend * tangent).astype(jnp.bfloat16))
+
+    token_terms = jnp.sum(project(vector) * (pulled * slopes), -1)
     demo_terms = jnp.sum(token_terms.reshape(-1, acts), -1)
-    owned = jnp.sum(swap(demo_terms.reshape(members, -1), ("zh", "y")), 0)
+    owned = jnp.sum(swap(demo_terms.reshape(16, -1), ("y", "zh")), 0)
     return (vector, -owned / (acts * math.sqrt(D * FF)))
 
 

time: 296 us -> 281 us (0.949)
  waiting for transfers between devices: 12.9 us -> 0 us
  blocking collectives: 250 us -> 258 us
  starting transfers between devices: 6.35 us -> 0 us
    all_gather x0 -> x4, blocking collectives: none -> 53.1 us  [the longest x1 26.7 us: shards(): stage = total(lax.all_gather(stage, 'zh', axis=0)).astype(jnp.bfloat16)]
    all_to_all x18 -> x14, blocking collectives: 250 us -> 204 us  [swap(): return lax.all_to_all(blocks, axes, 0, 0)]
    all_to_all x1 -> x0, waiting for transfers between devices: 12.9 us -> none  [swap(): return lax.all_to_all(blocks, axes, 0, 0)]
    all_to_all x1 -> x0, starting transfers between devices: 6.35 us -> none  [swap(): return lax.all_to_all(blocks, axes, 0, 0)]
  transfers between devices with their start and end apart: 1 -> 0, of which waited for: 1 -> 0; matrix products, arithmetic and copies ran while one was open for 0% -> 0% of each run, Pallas kernels for 0% -> 0%
where the time goes in v2:
time: 281 us; the launch traced here: 280 us
  blocking collectives  258 us (92%)
  matrix products  7.83 us (3%)
  other arithmetic  7.33 us (3%)
  local copies, waits for them, and re-layouts  3.66 us (1%)
  between operations  3.45 us (1%)
    all_to_all x14, blocking collectives, swap(): return lax.all_to_all(blocks, axes, 0, 0)  204 us
    all_gather x1, blocking collectives, shards(): stage = total(lax.all_gather(stage, 'zh', axis=0)).astype(jnp.bfloat16)  26.7 us
    all_gather x1, blocking collectives, shards(): both = lax.all_gather(jnp.stack([err, moved_err], 0), 'zh', axis=0)  18.4 us
    all_gather x2, blocking collectives, sum_copies(): return lax.all_gather(rows, 'c', axis=0, tiled=True)  7.99 us

profile of v2, /device:TPU:1, one launch (start us, length us, event | category | flops | bytes accessed | tf_op | source)
XLA Modules:
  0.0 279.9 jit_solution(8976960901829383801)
XLA Ops:
  1.4 1.0 fusion.17
  2.4 0.7 fusion.52
  3.2 0.8 fusion.38
  4.2 0.8 multiply_convert_fusion.5
  5.0 1.2 fusion.3
  6.7 28.2 %all_to_all.74 = bf16[4,16,1024]{2,1,0:T(8,128)(2,1)S(1)} all-to-all(bf16[4,16,1024]{2,1,0:T(8,128)(2,1)S(1)} %broadcast_in_dim.12), channel_id=1, replica_groups=mesh['zh'=4,'y'=4,'x'=4,'zl'=4,'c'=2] {'zh'}, dimensions={0} | all-to-all | bytes 262144 | tf_op jit(solution)/shard_map/all_to_all | solution.py:55
  35.0 10.9 %all_to_all.75 = bf16[4,4,16,1024]{3,2,1,0:T(8,128)(2,1)S(1)} all-to-all(bf16[4,4,16,1024]{3,2,1,0:T(8,128)(2,1)S(1)} %broadcast_in_dim.13), channel_id=1, replica_groups=mesh['zh'=4,'y'=4,'x'=4,'zl'=4,'c'=2] {'y'}, dimensions={0} | all-to-all | bytes 1048576 | tf_op jit(solution)/shard_map/all_to_all | solution.py:55
  46.2 0.7 copy-done.10
  46.9 1.0 multiply_convert_fusion.2
  48.5 13.1 %all_to_all.76 = bf16[4,4,2,16,1024]{4,3,2,1,0:T(8,128)(2,1)S(1)} all-to-all(bf16[4,4,2,16,1024]{4,3,2,1,0:T(8,128)(2,1)S(1)} %bitcast.97), channel_id=1, replica_groups=mesh['zh'=4,'y'=4,'x'=4,'zl'=4,'c'=2] {'y'}, dimensions={0} | all-to-all | bytes 2097152 | tf_op jit(solution)/shard_map/all_to_all | solution.py:55
  61.8 19.2 %all_to_all.77 = bf16[4,2,16,1024]{3,2,1,0:T(8,128)(2,1)S(1)} all-to-all(bf16[4,2,16,1024]{3,2,1,0:T(8,128)(2,1)S(1)} %reduce_sum.160), channel_id=1, replica_groups=mesh['zh'=4,'y'=4,'x'=4,'zl'=4,'c'=2] {'zh'}, dimensions={0} | all-to-all | bytes 524288 | tf_op jit(solution)/shard_map/all_to_all | solution.py:55
  81.1 18.4 %all-gather = bf16[8,16,1024]{2,1,0:T(8,128)(2,1)S(1)} all-gather(bf16[2,16,1024]{2,1,0:T(8,128)(2,1)S(1)} %pad_maximum_fusion.1), channel_id=2, replica_groups=mesh['zh'=4,'y'=4,'x'=4,'zl'=4,'c'=2] {'zh'}, dimensions={0}, use_global_device_ids=true | all-gather | bytes 327680 | tf_op jit(solution)/shard_map/all_gather | solution.py:113
  99.7 12.2 %all_to_all.78 = bf16[4,4,2,16,1024]{4,3,2,1,0:T(8,128)(2,1)S(1)} all-to-all(bf16[4,4,2,16,1024]{4,3,2,1,0:T(8,128)(2,1)S(1)} %broadcast_in_dim.14), channel_id=1, replica_groups=mesh['zh'=4,'y'=4,'x'=4,'zl'=4,'c'=2] {'y'}, dimensions={0} | all-to-all | bytes 2097152 | tf_op jit(solution)/shard_map/all_to_all | solution.py:55
  111.8 0.5 fusion.8
  112.4 0.9 copy-done.4
  113.4 0.9 fusion.23
  114.6 11.0 %all_to_all.79 = bf16[2,512,256]{2,1,0:T(8,128)(2,1)S(1)} all-to-all(bf16[2,512,256]{2,1,0:T(8,128)(2,1)S(1)} %bitcast.100), channel_id=1, replica_groups=mesh['zh'=4,'y'=4,'x'=4,'zl'=4,'c'=2] {'c'}, dimensions={0} | all-to-all | bytes 1048576 | tf_op jit(solution)/shard_map/all_to_all | solution.py:55
  125.8 20.3 %all_to_all.80 = bf16[16,32,256]{2,1,0:T(8,128)(2,1)S(1)} all-to-all(bf16[16,32,256]{2,1,0:T(8,128)(2,1)S(1)} %bitcast.108), channel_id=1, replica_groups=mesh['zh'=4,'y'=4,'x'=4,'zl'=4,'c'=2] {'x','zl'}, dimensions={0} | all-to-all | bytes 524288 | tf_op jit(solution)/shard_map/all_to_all | solution.py:55
  146.2 13.1 %all_to_all.81 = bf16[16,32,256]{2,1,0:T(8,128)(2,1)S(1)} all-to-all(bf16[16,32,256]{2,1,0:T(8,128)(2,1)S(1)} %broadcast_in_dim.15), channel_id=1, replica_groups=mesh['zh'=4,'y'=4,'x'=4,'zl'=4,'c'=2] {'x','zl'}, dimensions={0} | all-to-all | bytes 524288 | tf_op jit(solution)/shard_map/all_to_all | solution.py:55
  159.3 4.0 %all_gather.20 = bf16[1024,256]{1,0:T(8,128)(2,1)S(1)} all-gather(bf16[512,256]{1,0:T(8,128)(2,1)S(1)} %bitcast.103), channel_id=1, replica_groups=mesh['zh'=4,'y'=4,'x'=4,'zl'=4,'c'=2] {'c'}, dimensions={0}, use_global_device_ids=true | all-gather | bytes 786432 | tf_op jit(solution)/shard_map/all_gather | solution.py:72
  164.4 11.6 %all_to_all.82 = bf16[4,64,1024]{2,1,0:T(8,128)(2,1)S(1)} all-to-all(bf16[4,64,1024]{2,1,0:T(8,128)(2,1)S(1)} %bitcast.112), channel_id=1, replica_groups=mesh['zh'=4,'y'=4,'x'=4,'zl'=4,'c'=2] {'y'}, dimensions={0} | all-to-all | bytes 1048576 | tf_op jit(solution)/shard_map/all_to_all | solution.py:55
  176.1 26.7 %all-gather.1 = bf16[256,1024]{1,0:T(8,128)(2,1)S(1)} all-gather(bf16[64,1024]{1,0:T(8,128)(2,1)S(1)} %reduce_sum.164), channel_id=3, replica_groups=mesh['zh'=4,'y'=4,'x'=4,'zl'=4,'c'=2] {'zh'}, dimensions={0}, use_global_device_ids=true | all-gather | bytes 655360 | tf_op jit(solution)/shard_map/all_gather | solution.py:124
  202.9 10.2 %all_to_all.83 = bf16[4,64,1024]{2,1,0:T(8,128)(2,1)S(1)} all-to-all(bf16[4,64,1024]{2,1,0:T(8,128)(2,1)S(1)} %broadcast_in_dim.16), channel_id=1, replica_groups=mesh['zh'=4,'y'=4,'x'=4,'zl'=4,'c'=2] {'y'}, dimensions={0} | all-to-all | bytes 1048576 | tf_op jit(solution)/shard_map/all_to_all | solution.py:55
  213.2 2.7 convolution_convert_fusion.1
  215.9 7.5 %all_to_all.84 = bf16[2,512,256]{2,1,0:T(8,128)(2,1)S(1)} all-to-all(bf16[2,512,256]{2,1,0:T(8,128)(2,1)} %bitcast.111), channel_id=1, replica_groups=mesh['zh'=4,'y'=4,'x'=4,'zl'=4,'c'=2] {'c'}, dimensions={0} | all-to-all | bytes 1048576 | tf_op jit(solution)/shard_map/all_to_all | solution.py:55
  223.4 0.8 reduce_sum.166
  224.2 13.5 %all_to_all.85 = bf16[16,32,256]{2,1,0:T(8,128)(2,1)S(1)} all-to-all(bf16[16,32,256]{2,1,0:T(8,128)(2,1)} %bitcast.109), channel_id=1, replica_groups=mesh['zh'=4,'y'=4,'x'=4,'zl'=4,'c'=2] {'x','zl'}, dimensions={0} | all-to-all | bytes 524288 | tf_op jit(solution)/shard_map/all_to_all | solution.py:55
  237.8 13.3 %all_to_all.86 = bf16[16,32,256]{2,1,0:T(8,128)(2,1)S(1)} all-to-all(bf16[16,32,256]{2,1,0:T(8,128)(2,1)S(1)} %broadcast_in_dim.17), channel_id=1, replica_groups=mesh['zh'=4,'y'=4,'x'=4,'zl'=4,'c'=2] {'x','zl'}, dimensions={0} | all-to-all | bytes 524288 | tf_op jit(solution)/shard_map/all_to_all | solution.py:55
  251.0 4.0 %all_gather.23 = bf16[1024,256]{1,0:T(8,128)(2,1)S(1)} all-gather(bf16[512,256]{1,0:T(8,128)(2,1)S(1)} %bitcast.104), channel_id=1, replica_groups=mesh['zh'=4,'y'=4,'x'=4,'zl'=4,'c'=2] {'c'}, dimensions={0}, use_global_device_ids=true | all-gather | bytes 786432 | tf_op jit(solution)/shard_map/all_gather | solution.py:72
  255.3 1.0 copy-done.2
  257.0 20.5 %all_to_all.87 = f32[16,1,1]{2,1,0:T(1,128)S(1)} all-to-all(f32[16,1,1]{2,1,0:T(1,128)S(1)} %copy.28), channel_id=1, replica_groups=mesh['zh'=4,'y'=4,'x'=4,'zl'=4,'c'=2] {'y','zh'}, dimensions={0} | all-to-all | bytes 128 | tf_op jit(solution)/shard_map/all_to_all | solution.py:55
  277.5 0.6 reduce_sum.170
  (58 shorter events, 5.1 us)
Async XLA Ops:
  0.6 47.4 %copy-start = (bf16[256,1024]{1,0:T(8,128)(2,1)S(1)}, bf16[256,1024]{1,0:T(8,128)(2,1)}, u32[]{:S(2)}) copy-start(bf16[256,1024]{1,0:T(8,128)(2,1)} %param.14) | copy-start | bytes 1572868
  0.6 5.6 %copy-start.9 = (bf16[2,1,256,256]{3,2,1,0:T(8,128)(2,1)S(1)}, bf16[2,1,256,256]{3,2,1,0:T(8,128)(2,1)}, u32[]{:S(2)}) copy-start(bf16[2,1,256,256]{3,2,1,0:T(8,128)(2,1)} %param.10) | copy-start | bytes 786436
  0.7 5.8 %copy-start.5 = (bf16[16,1024]{1,0:T(8,128)(2,1)S(1)}, bf16[16,1024]{1,0:T(8,128)(2,1)}, u32[]{:S(2)}) copy-start(bf16[16,1024]{1,0:T(8,128)(2,1)} %param.9) | copy-start | bytes 98308
  0.7 5.8 %copy-start.6 = (bf16[16,1024]{1,0:T(8,128)(2,1)S(1)}, bf16[16,1024]{1,0:T(8,128)(2,1)}, u32[]{:S(2)}) copy-start(bf16[16,1024]{1,0:T(8,128)(2,1)} %param.8) | copy-start | bytes 98308
  6.7 39.2 %copy-start.1 = (f32[1024,256]{1,0:T(8,128)S(1)}, f32[1024,256]{1,0:T(8,128)}, u32[]{:S(2)}) copy-start(f32[1024,256]{1,0:T(8,128)} %param.15) | copy-start | bytes 3145732
  45.9 1.0 copy-start.10
  46.9 1.0 copy-start.3
  112.3 1.0 copy-start.4
  112.3 1.0 copy-start.8
  163.7 0.7 copy-start.7
  255.3 1.0 copy-start.2

commit v3 on v2

--- a/solution.py
+++ b/solution.py
@@ -63,11 +63,11 @@
     return jnp.sum(blocks.astype(jnp.float32), 0)
 
 
-def sum_copies(part):
-    columns = part.shape[1]
-    half = D // 2
-    pair = total(swap(part.astype(jnp.bfloat16).reshape(2, half, columns), "c"))
-    rows = total(swap(pair.astype(jnp.bfloat16).reshape(16, half // 16, columns), GRID))
+def sum_copies(kept, given):
+    half, columns = kept.shape
+    taken = lax.ppermute(given.astype(jnp.bfloat16), "c", [(0, 1), (1, 0)])
+    pair = (kept + taken.astype(jnp.float32)).astype(jnp.bfloat16)
+    rows = total(swap(pair.reshape(16, half // 16, columns), GRID))
     rows = collect(rows.astype(jnp.bfloat16), GRID, 16).reshape(half, columns)
     return lax.all_gather(rows, "c", axis=0, tiled=True)
 
@@ -90,11 +90,17 @@
     def project(vector):
         return jnp.dot(gathered, vector.astype(jnp.bfloat16), preferred_element_type=jnp.float32)
 
+    core = lax.axis_index("c")
+    mine = lax.dynamic_slice_in_dim(gathered, core * (D // 2), D // 2, 1)
+    other = lax.dynamic_slice_in_dim(gathered, (1 - core) * (D // 2), D // 2, 1)
+
+    def outer(features, second):
+        return lax.dot_general(
+            features, second, (((0,), (0,)), ((), ())), preferred_element_type=jnp.float32
+        )
+
     def hvp(second):
-        part = lax.dot_general(
-            gathered, second, (((0,), (0,)), ((), ())), preferred_element_type=jnp.float32
-        )
-        return sum_copies(part).astype(jnp.float32) / count
+        return sum_copies(outer(mine, second), outer(other, second)).astype(jnp.float32) / count
 
     units = w_up.shape[1]
     pre = jnp.dot(gathered, w_up, preferred_element_type=jnp.float32)

time: 281 us -> 277 us (0.986)
  blocking collectives: 258 us -> 226 us
  starting transfers between devices: 0 us -> 17.1 us
  waiting for transfers between devices: 0 us -> 12 us
    all_to_all x14 -> x11, blocking collectives: 204 us -> 174 us  [swap(): return lax.all_to_all(blocks, axes, 0, 0)]
    ppermute x0 -> x2, starting transfers between devices: none -> 13.6 us  [sum_copies(): taken = lax.ppermute(given.astype(jnp.bfloat16), 'c', [(0, 1), (1, 0)])]
    all_to_all x0 -> x1, waiting for transfers between devices: none -> 9.7 us  [swap(): return lax.all_to_all(blocks, axes, 0, 0)]
    all_to_all x0 -> x1, starting transfers between devices: none -> 3.52 us  [swap(): return lax.all_to_all(blocks, axes, 0, 0)]
  transfers between devices with their start and end apart: 0 -> 3, of which waited for: 0 -> 3; matrix products, arithmetic and copies ran while one was open for 0% -> 0% of each run, Pallas kernels for 0% -> 0%
where the time goes in v3:
time: 277 us; the launch traced here: 276 us
  blocking collectives  226 us (82%)
  starting transfers between devices  17.1 us (6%)
  waiting for transfers between devices  12 us (4%)
  matrix products  6.17 us (2%)
  other arithmetic  5.58 us (2%)
  local copies, waits for them, and re-layouts  5.22 us (2%)
  between operations  3.53 us (1%)
    all_to_all x11, blocking collectives, swap(): return lax.all_to_all(blocks, axes, 0, 0)  174 us
    all_gather x1, blocking collectives, shards(): stage = total(lax.all_gather(stage, 'zh', axis=0)).astype(jnp.bfloat16)  26.4 us
    all_gather x1, blocking collectives, shards(): both = lax.all_gather(jnp.stack([err, moved_err], 0), 'zh', axis=0)  18.4 us
    ppermute x2, starting transfers between devices, sum_copies(): taken = lax.ppermute(given.astype(jnp.bfloat16), 'c', [(0, 1), (1, 0)])  13.6 us
    all_to_all x1, waiting for transfers between devices, swap(): return lax.all_to_all(blocks, axes, 0, 0)  9.7 us
    all_gather x2, blocking collectives, sum_copies(): return lax.all_gather(rows, 'c', axis=0, tiled=True)  7.99 us
  transfers between devices with their start and end apart: 3, of which 3 were waited for; matrix products, arithmetic and copies ran while one was open for 0% of the time, Pallas kernels for 0%

profile of v3, /device:TPU:1, one launch (start us, length us, event | category | flops | bytes accessed | tf_op | source)
XLA Modules:
  0.0 275.9 jit_solution(17167780068322355849)
XLA Ops:
  1.4 0.8 fusion.47
  2.5 0.8 multiply_convert_fusion.5
  3.3 1.0 fusion.17
  4.3 1.2 fusion.3
  6.0 28.2 %all_to_all.64 = bf16[4,16,1024]{2,1,0:T(8,128)(2,1)S(1)} all-to-all(bf16[4,16,1024]{2,1,0:T(8,128)(2,1)S(1)} %broadcast_in_dim.12), channel_id=1, replica_groups=mesh['zh'=4,'y'=4,'x'=4,'zl'=4,'c'=2] {'zh'}, dimensions={0} | all-to-all | bytes 262144 | tf_op jit(solution)/shard_map/all_to_all | solution.py:55
  34.3 10.9 %all_to_all.65 = bf16[4,4,16,1024]{3,2,1,0:T(8,128)(2,1)S(1)} all-to-all(bf16[4,4,16,1024]{3,2,1,0:T(8,128)(2,1)S(1)} %broadcast_in_dim.13), channel_id=1, replica_groups=mesh['zh'=4,'y'=4,'x'=4,'zl'=4,'c'=2] {'y'}, dimensions={0} | all-to-all | bytes 1048576 | tf_op jit(solution)/shard_map/all_to_all | solution.py:55
  45.5 0.7 copy-done.14
  46.2 1.0 multiply_convert_fusion.2
  47.7 13.1 %all_to_all.66 = bf16[4,4,2,16,1024]{4,3,2,1,0:T(8,128)(2,1)S(1)} all-to-all(bf16[4,4,2,16,1024]{4,3,2,1,0:T(8,128)(2,1)S(1)} %bitcast.98), channel_id=1, replica_groups=mesh['zh'=4,'y'=4,'x'=4,'zl'=4,'c'=2] {'y'}, dimensions={0} | all-to-all | bytes 2097152 | tf_op jit(solution)/shard_map/all_to_all | solution.py:55
  61.0 19.2 %all_to_all.67 = bf16[4,2,16,1024]{3,2,1,0:T(8,128)(2,1)S(1)} all-to-all(bf16[4,2,16,1024]{3,2,1,0:T(8,128)(2,1)S(1)} %reduce_sum.136), channel_id=1, replica_groups=mesh['zh'=4,'y'=4,'x'=4,'zl'=4,'c'=2] {'zh'}, dimensions={0} | all-to-all | bytes 524288 | tf_op jit(solution)/shard_map/all_to_all | solution.py:55
  80.4 18.4 %all-gather = bf16[8,16,1024]{2,1,0:T(8,128)(2,1)S(1)} all-gather(bf16[2,16,1024]{2,1,0:T(8,128)(2,1)S(1)} %pad_maximum_fusion.1), channel_id=2, replica_groups=mesh['zh'=4,'y'=4,'x'=4,'zl'=4,'c'=2] {'zh'}, dimensions={0}, use_global_device_ids=true | all-gather | bytes 327680 | tf_op jit(solution)/shard_map/all_gather | solution.py:119
  98.8 1.1 broadcast_in_dim.14
  99.9 3.5 %all-to-all-start.4 = ((bf16[4,4,2,16,1024]{4,3,2,1,0:T(8,128)(2,1)}), bf16[4,4,2,16,1024]{4,3,2,1,0:T(8,128)(2,1)S(1)}, u32[]{:S(2)}, u32[]{:S(2)}) async-start(bf16[4,4,2,16,1024]{4,3,2,1,0:T(8,128)(2,1)} %broadcast_in_dim.14), calls=%async_computation.4 | async-start | bytes 2097152 | tf_op jit(solution)/shard_map/all_to_all | solution.py:55
  103.4 9.7 %all-to-all-done.4 = bf16[4,4,2,16,1024]{4,3,2,1,0:T(8,128)(2,1)S(1)} async-done(((bf16[4,4,2,16,1024]{4,3,2,1,0:T(8,128)(2,1)}), bf16[4,4,2,16,1024]{4,3,2,1,0:T(8,128)(2,1)S(1)}, u32[]{:S(2)}, u32[]{:S(2)}) %all-to-all-start.4) | async-done | bytes 1048608 | tf_op jit(solution)/shard_map/all_to_all | solution.py:55
  113.7 0.9 copy-done.4
  114.6 0.9 fusion.23
  115.8 9.2 %collective-permute-start = (bf16[512,256]{1,0:T(8,128)(2,1)S(1)}, bf16[512,256]{1,0:T(8,128)(2,1)S(1)}, u32[]{:S(2)}, u32[]{:S(2)}) collective-permute-start(bf16[512,256]{1,0:T(8,128)(2,1)S(1)} %convolution_convert_fusion.3), channel_id=1, source_target_pairs={{0,1},{1,0},{2,3},{3,2},{4,5},{5,4},{6,7},{7,6},{8,9},{9,8},{10,11... | collective-permute-start | bytes 786440 | tf_op jit(solution)/shard_map/ppermute | solution.py:68
  125.0 1.1 collective-permute-done
  126.4 20.3 %all_to_all.68 = bf16[16,32,256]{2,1,0:T(8,128)(2,1)S(1)} all-to-all(bf16[16,32,256]{2,1,0:T(8,128)(2,1)S(1)} %bitcast.104), channel_id=1, replica_groups=mesh['zh'=4,'y'=4,'x'=4,'zl'=4,'c'=2] {'x','zl'}, dimensions={0} | all-to-all | bytes 524288 | tf_op jit(solution)/shard_map/all_to_all | solution.py:55
  146.8 13.1 %all_to_all.69 = bf16[16,32,256]{2,1,0:T(8,128)(2,1)S(1)} all-to-all(bf16[16,32,256]{2,1,0:T(8,128)(2,1)S(1)} %broadcast_in_dim.15), channel_id=1, replica_groups=mesh['zh'=4,'y'=4,'x'=4,'zl'=4,'c'=2] {'x','zl'}, dimensions={0} | all-to-all | bytes 524288 | tf_op jit(solution)/shard_map/all_to_all | solution.py:55
  159.9 4.0 %all_gather.20 = bf16[1024,256]{1,0:T(8,128)(2,1)S(1)} all-gather(bf16[512,256]{1,0:T(8,128)(2,1)S(1)} %bitcast.105), channel_id=1, replica_groups=mesh['zh'=4,'y'=4,'x'=4,'zl'=4,'c'=2] {'c'}, dimensions={0}, use_global_device_ids=true | all-gather | bytes 786432 | tf_op jit(solution)/shard_map/all_gather | solution.py:72
  165.6 11.6 %all_to_all.70 = bf16[4,64,1024]{2,1,0:T(8,128)(2,1)S(1)} all-to-all(bf16[4,64,1024]{2,1,0:T(8,128)(2,1)S(1)} %bitcast.111), channel_id=1, replica_groups=mesh['zh'=4,'y'=4,'x'=4,'zl'=4,'c'=2] {'y'}, dimensions={0} | all-to-all | bytes 1048576 | tf_op jit(solution)/shard_map/all_to_all | solution.py:55
  177.3 26.4 %all-gather.1 = bf16[256,1024]{1,0:T(8,128)(2,1)S(1)} all-gather(bf16[64,1024]{1,0:T(8,128)(2,1)S(1)} %reduce_sum.139), channel_id=3, replica_groups=mesh['zh'=4,'y'=4,'x'=4,'zl'=4,'c'=2] {'zh'}, dimensions={0}, use_global_device_ids=true | all-gather | bytes 655360 | tf_op jit(solution)/shard_map/all_gather | solution.py:130
  203.9 10.4 %all_to_all.71 = bf16[4,64,1024]{2,1,0:T(8,128)(2,1)S(1)} all-to-all(bf16[4,64,1024]{2,1,0:T(8,128)(2,1)S(1)} %broadcast_in_dim.16), channel_id=1, replica_groups=mesh['zh'=4,'y'=4,'x'=4,'zl'=4,'c'=2] {'y'}, dimensions={0} | all-to-all | bytes 1048576 | tf_op jit(solution)/shard_map/all_to_all | solution.py:55
  215.0 4.5 %collective-permute-start.1 = (bf16[512,256]{1,0:T(8,128)(2,1)S(1)}, bf16[512,256]{1,0:T(8,128)(2,1)S(1)}, u32[]{:S(2)}, u32[]{:S(2)}) collective-permute-start(bf16[512,256]{1,0:T(8,128)(2,1)S(1)} %convolution_convert_fusion.2), channel_id=1, source_target_pairs={{0,1},{1,0},{2,3},{3,2},{4,5},{5,4},{6,7},{7,6},{8,9},{9,8},{10,11... | collective-permute-start | bytes 786440 | tf_op jit(solution)/shard_map/ppermute | solution.py:68
  219.4 1.1 collective-permute-done.1
  220.9 12.6 %all_to_all.72 = bf16[16,32,256]{2,1,0:T(8,128)(2,1)S(1)} all-to-all(bf16[16,32,256]{2,1,0:T(8,128)(2,1)S(1)} %bitcast.102), channel_id=1, replica_groups=mesh['zh'=4,'y'=4,'x'=4,'zl'=4,'c'=2] {'x','zl'}, dimensions={0} | all-to-all | bytes 524288 | tf_op jit(solution)/shard_map/all_to_all | solution.py:55
  233.5 13.3 %all_to_all.73 = bf16[16,32,256]{2,1,0:T(8,128)(2,1)S(1)} all-to-all(bf16[16,32,256]{2,1,0:T(8,128)(2,1)S(1)} %broadcast_in_dim.17), channel_id=1, replica_groups=mesh['zh'=4,'y'=4,'x'=4,'zl'=4,'c'=2] {'x','zl'}, dimensions={0} | all-to-all | bytes 524288 | tf_op jit(solution)/shard_map/all_to_all | solution.py:55
  246.8 4.0 %all_gather.23 = bf16[1024,256]{1,0:T(8,128)(2,1)S(1)} all-gather(bf16[512,256]{1,0:T(8,128)(2,1)S(1)} %bitcast.106), channel_id=1, replica_groups=mesh['zh'=4,'y'=4,'x'=4,'zl'=4,'c'=2] {'c'}, dimensions={0}, use_global_device_ids=true | all-gather | bytes 786432 | tf_op jit(solution)/shard_map/all_gather | solution.py:72
  251.1 1.0 copy-done.2
  252.8 20.8 %all_to_all.74 = f32[16,1,1]{2,1,0:T(1,128)S(1)} all-to-all(f32[16,1,1]{2,1,0:T(1,128)S(1)} %copy.28), channel_id=1, replica_groups=mesh['zh'=4,'y'=4,'x'=4,'zl'=4,'c'=2] {'y','zh'}, dimensions={0} | all-to-all | bytes 128 | tf_op jit(solution)/shard_map/all_to_all | solution.py:55
  273.5 0.6 reduce_sum.144
  (72 shorter events, 7.0 us)
Async XLA Ops:
  0.6 46.7 %copy-start = (bf16[256,1024]{1,0:T(8,128)(2,1)S(1)}, bf16[256,1024]{1,0:T(8,128)(2,1)}, u32[]{:S(2)}) copy-start(bf16[256,1024]{1,0:T(8,128)(2,1)} %param.14) | copy-start | bytes 1572868
  0.6 5.1 %copy-start.6 = (bf16[16,1024]{1,0:T(8,128)(2,1)S(1)}, bf16[16,1024]{1,0:T(8,128)(2,1)}, u32[]{:S(2)}) copy-start(bf16[16,1024]{1,0:T(8,128)(2,1)} %param.8) | copy-start | bytes 98308
  0.7 5.1 %copy-start.5 = (bf16[16,1024]{1,0:T(8,128)(2,1)S(1)}, bf16[16,1024]{1,0:T(8,128)(2,1)}, u32[]{:S(2)}) copy-start(bf16[16,1024]{1,0:T(8,128)(2,1)} %param.9) | copy-start | bytes 98308
  0.7 4.8 %copy-start.13 = (bf16[2,1,256,256]{3,2,1,0:T(8,128)(2,1)S(1)}, bf16[2,1,256,256]{3,2,1,0:T(8,128)(2,1)}, u32[]{:S(2)}) copy-start(bf16[2,1,256,256]{3,2,1,0:T(8,128)(2,1)} %param.10) | copy-start | bytes 786436
  0.7 5.2 %copy-start.15 = (s32[16]{0:T(128)S(1)}, s32[16]{0:T(128)}, u32[]{:S(2)}) copy-start(s32[16]{0:T(128)} %param.12) | copy-start | bytes 196
  6.0 39.2 %copy-start.1 = (f32[1024,256]{1,0:T(8,128)S(1)}, f32[1024,256]{1,0:T(8,128)}, u32[]{:S(2)}) copy-start(f32[1024,256]{1,0:T(8,128)} %param.15) | copy-start | bytes 3145732
  45.2 1.0 copy-start.14
  46.2 1.0 copy-start.3
  99.9 13.2 %all-to-all-start.4 = ((bf16[4,4,2,16,1024]{4,3,2,1,0:T(8,128)(2,1)}), bf16[4,4,2,16,1024]{4,3,2,1,0:T(8,128)(2,1)S(1)}, u32[]{:S(2)}, u32[]{:S(2)}) async-start(bf16[4,4,2,16,1024]{4,3,2,1,0:T(8,128)(2,1)} %broadcast_in_dim.14), calls=%async_computation.4 | async-start | bytes 2097152 | tf_op jit(solution)/shard_map/all_to_all | solution.py:55
  113.6 1.0 copy-start.4
  113.6 1.0 copy-start.9
  115.8 10.3 %collective-permute-start = (bf16[512,256]{1,0:T(8,128)(2,1)S(1)}, bf16[512,256]{1,0:T(8,128)(2,1)S(1)}, u32[]{:S(2)}, u32[]{:S(2)}) collective-permute-start(bf16[512,256]{1,0:T(8,128)(2,1)S(1)} %convolution_convert_fusion.3), channel_id=1, source_target_pairs={{0,1},{1,0},{2,3},{3,2},{4,5},{5,4},{6,7},{7,6},{8,9},{9,8},{10,11... | collective-permute-start | bytes 786440 | tf_op jit(solution)/shard_map/ppermute | solution.py:68
  164.0 0.9 copy-start.10
  164.9 0.7 copy-start.7
  203.8 10.5 %copy-start.8 = (f32[256,256]{1,0:T(8,128)S(1)}, f32[256,256]{1,0:T(8,128)}, u32[]{:S(2)}) copy-start(f32[256,256]{1,0:T(8,128)} %copy-done.7) | copy-start | bytes 786436
  203.8 10.5 %copy-start.11 = (f32[256,256]{1,0:T(8,128)S(1)}, f32[256,256]{1,0:T(8,128)}, u32[]{:S(2)}) copy-start(f32[256,256]{1,0:T(8,128)} %get-tuple-element.11) | copy-start | bytes 786436
  203.8 10.5 %copy-start.12 = (f32[256,256]{1,0:T(8,128)S(1)}, f32[256,256]{1,0:T(8,128)}, u32[]{:S(2)}) copy-start(f32[256,256]{1,0:T(8,128)} %get-tuple-element.3) | copy-start | bytes 786436
  215.0 5.6 %collective-permute-start.1 = (bf16[512,256]{1,0:T(8,128)(2,1)S(1)}, bf16[512,256]{1,0:T(8,128)(2,1)S(1)}, u32[]{:S(2)}, u32[]{:S(2)}) collective-permute-start(bf16[512,256]{1,0:T(8,128)(2,1)S(1)} %convolution_convert_fusion.2), channel_id=1, source_target_pairs={{0,1},{1,0},{2,3},{3,2},{4,5},{5,4},{6,7},{7,6},{8,9},{9,8},{10,11... | collective-permute-start | bytes 786440 | tf_op jit(solution)/shard_map/ppermute | solution.py:68
  251.1 1.0 copy-start.2

commit v4 on v3

v4 whole, which is shorter than its diff:
```python
import functools
import math

import jax
import jax.numpy as jnp
from jax import lax
from jax.experimental import pallas as pl
from jax.experimental.pallas import tpu as pltpu
from jax.sharding import Mesh
from jax.sharding import PartitionSpec as P

D = 1024
FF = 4096
STEPS_T = 10
TOKENS = 8192

epsilon = 1e-06
sharpness_divisor = 6.0
damping_factor = 0.01
rest = 1.0 - damping_factor
keep = 1.0 + rest

AXES = ("zh", "y", "x", "zl", "c")
SIZES = (4, 4, 4, 4, 2)
GRID = ("x", "zl")

SCALARS = pl.BlockSpec(memory_space=pltpu.SMEM)
BLOCK = pl.BlockSpec(memory_space=pltpu.VMEM)


def local(kernel, specs, outs):
    return pl.pallas_call(
        kernel,
        in_specs=specs,
        out_specs=[BLOCK] * len(outs),
        out_shape=[jax.ShapeDtypeStruct(shape, dtype) for shape, dtype in outs],
        compiler_params=pltpu.CompilerParams(vmem_limit_bytes=24 * 2**20),
    )


def nn(left, right):
    return jnp.dot(left, right, preferred_element_type=jnp.float32)


def nt(left, right):
    return lax.dot_general(
        left, right, (((1,), (1,)), ((), ())), preferred_element_type=jnp.float32
    )


def tn(left, right):
    return lax.dot_general(
        left, right, (((0,), (0,)), ((), ())), preferred_element_type=jnp.float32
    )


def attend(flow_ref, mask_ref, noise_ref, action_ref, kv_ref, sent_ref, resid_ref):
    acts, width = noise_ref.shape
    span = kv_ref.shape[3]
    heads = width // span
    time = (flow_ref[0].astype(jnp.float32) + 1.0) / (STEPS_T + 1.0)
    row = lax.broadcasted_iota(jnp.int32, (acts, 128), 0)
    mask = jnp.zeros((acts, 128), jnp.float32)
    for i in range(acts):
        mask = jnp.where(row == i, mask_ref[i].astype(jnp.float32), mask)
    mask = mask[:, :1]
    noisy = noise_ref[...].astype(jnp.float32)
    clean = action_ref[...].astype(jnp.float32)
    inputs = time * noisy + (1.0 - time) * clean
    queries = jnp.concatenate([inputs[:, i * span : (i + 1) * span] for i in range(heads)], 0)
    queries = queries * lax.rsqrt(jnp.mean(queries * queries, -1, keepdims=True) + epsilon)
    keys = kv_ref[0, 0].astype(jnp.float32)
    keys = keys * lax.rsqrt(jnp.mean(keys * keys, -1, keepdims=True) + epsilon)
    energies = nt(queries.astype(jnp.bfloat16), keys.astype(jnp.bfloat16))
    expo = jnp.exp(energies * (sharpness_divisor / span))
    weights = (expo / jnp.sum(expo, -1, keepdims=True)).astype(jnp.bfloat16)
    mixed = nn(weights, kv_ref[1, 0])
    mixed = jnp.concatenate([mixed[i * acts : (i + 1) * acts] for i in range(heads)], 1)
    hidden = inputs + mixed
    normed = hidden * lax.rsqrt(jnp.mean(hidden * hidden, -1, keepdims=True) + epsilon)
    normed = (normed.astype(jnp.bfloat16).astype(jnp.float32) * mask).astype(jnp.bfloat16)
    for i in range(sent_ref.shape[0]):
        sent_ref[i] = normed
    resid_ref[...] = mask * (hidden - (noisy - clean))


def forward(rows_ref, up_ref, query_ref, lin_ref, slopes_ref, curves_ref, tangent_ref):
    rows = rows_ref[...]
    pre = nn(rows, up_ref[...])
    sig = jax.nn.sigmoid(pre)
    slopes = sig * (1.0 + pre * (1.0 - sig))
    curves_ref[...] = sig * (1.0 - sig) * (2.0 + pre * (1.0 - 2.0 * sig))
    tangent = nn(rows, query_ref[...].astype(jnp.bfloat16))
    slopes_ref[...] = slopes
    tangent_ref[...] = tangent
    active = (pre * sig).astype(jnp.bfloat16)
    linear = (slopes * tangent).astype(jnp.bfloat16)
    lin_ref[:, :, 0] = active.reshape(4, 4, 16, -1)
    lin_ref[:, :, 1] = linear.reshape(4, 4, 16, -1)


def down(lin_ref, *refs):
    *blocks, out_ref = refs
    place = lax.axis_index("y")
    rows = out_ref.shape[0]
    out = 0.0
    for j, block in enumerate(blocks):
        source = lin_ref[lax.rem(place + j, 4)].reshape(rows, -1)
        out = out + nn(source, block[...])
    out_ref[...] = out.astype(jnp.bfloat16)


def pull(source_ref, *refs):
    *blocks, out_ref = refs
    place = lax.axis_index("y")
    if source_ref.ndim == 3:
        source = source_ref[0].astype(jnp.float32)
        for i in range(1, source_ref.shape[0]):
            source = source + source_ref[i].astype(jnp.float32)
        source = source.astype(jnp.bfloat16)
    else:
        source = source_ref[...]
    for j, block in enumerate(blocks):
        out_ref[lax.rem(place + j, 4)] = nt(source, block[...]).astype(jnp.bfloat16)


def halves(rows_ref, second, kept_ref, given_ref):
    half = D // 2
    low = tn(rows_ref[:, :half], second).astype(jnp.bfloat16)
    high = tn(rows_ref[:, half:], second).astype(jnp.bfloat16)
    core = lax.axis_index("c")

    @pl.when(core == 0)
    def _():
        kept_ref[...] = low
        given_ref[...] = high

    @pl.when(core == 1)
    def _():
        kept_ref[...] = high
        given_ref[...] = low


def curve_first(
    both_ref, slopes_ref, curves_ref, tangent_ref, rows_ref, kept_ref, given_ref, bend_ref, back_ref
):
    shape = slopes_ref.shape
    pulled = both_ref[:, :, 0].reshape(shape).astype(jnp.float32)
    moved = both_ref[:, :, 1].reshape(shape).astype(jnp.float32)
    slopes = slopes_ref[...]
    bend = pulled * curves_ref[...]
    bend_ref[...] = bend
    back_ref[...] = pulled * slopes
    second = (moved * slopes + bend * tangent_ref[...]).astype(jnp.bfloat16)
    halves(rows_ref, second, kept_ref, given_ref)


def turn(rows_ref, first_ref, slopes_ref, tangent_ref, lin_ref, along_ref):
    along = nn(rows_ref[...], first_ref[...]) / TOKENS
    along_ref[...] = along
    later = keep * tangent_ref[...] - along
    lin_ref[...] = (slopes_ref[...] * later).astype(jnp.bfloat16).reshape(lin_ref.shape)


def curve_second(
    moved_ref, slopes_ref, bend_ref, tangent_ref, along_ref, rows_ref, kept_ref, given_ref
):
    moved = moved_ref[...].reshape(slopes_ref.shape).astype(jnp.float32)
    later = keep * tangent_ref[...] - along_ref[...]
    second = (moved * slopes_ref[...] + bend_ref[...] * later).astype(jnp.bfloat16)
    halves(rows_ref, second, kept_ref, given_ref)


def score(rows_ref, second_ref, tangent_ref, along_ref, back_ref, terms_ref):
    along = nn(rows_ref[...], second_ref[...]) / TOKENS
    projected = (1.0 + rest * keep) * tangent_ref[...] - rest * along_ref[...] - along
    terms = (projected * back_ref[...]).reshape(16, 2, 8, 256)
    terms = terms[:, 0] + terms[:, 1]
    terms_ref[...] = terms[:, :, :128] + terms[:, :, 128:]


def swap(blocks, axes):
    return lax.all_to_all(blocks, axes, 0, 0)


def collect(block, axes, members):
    return swap(jnp.broadcast_to(block[None], (members, *block.shape)), axes)


def total(blocks):
    return jnp.sum(blocks.astype(jnp.float32), 0)


def sum_copies(kept, given):
    half, columns = kept.shape
    taken = lax.ppermute(given, "c", [(0, 1), (1, 0)])
    pair = (kept.astype(jnp.float32) + taken.astype(jnp.float32)).astype(jnp.bfloat16)
    rows = total(swap(pair.reshape(16, half // 16, columns), GRID))
    rows = collect(rows.astype(jnp.bfloat16), GRID, 16).reshape(half, columns)
    return lax.all_gather(rows, "c", axis=0, tiled=True)


def shards(noise_embed, action_embed, prefix_kv, flow_step, action_mask, w_up, w_down, query_grad):
    own = noise_embed.shape[0]
    tokens = own * 16
    units = w_up.shape[1]
    half = jnp.bfloat16
    full = jnp.float32
    square = ((tokens, units), full)
    blocks = [w_down]
    for shift in (1, 2, 3):
        blocks.append(lax.ppermute(w_down, "y", [((i + shift) % 4, i) for i in range(4)]))

    sent, resid = local(
        attend,
        [SCALARS, SCALARS, BLOCK, BLOCK, BLOCK],
        [((4, own, D), half), ((own, D), full)],
    )(flow_step, action_mask, noise_embed, action_embed, prefix_kv)
    stage, blocks = lax.optimization_barrier((swap(sent, "zh"), blocks))
    rows = collect(stage, "y", 4).reshape(tokens, D)
    lin, slopes, curves, tangent = local(
        forward, [BLOCK] * 3, [((4, 4, 2, own, units), half), square, square, square]
    )(rows, w_up, query_grad)
    (stage,) = local(down, [BLOCK] * 5, [((8 * own, D), half)])(swap(lin, "y"), *blocks)
    both = total(swap(stage.reshape(4, 2, own, D), "zh"))
    both = jnp.stack([(resid + both[0]).astype(half), both[1].astype(half)])
    both = lax.all_gather(both, "zh", axis=0).reshape(8 * own, D)
    (both,) = local(pull, [BLOCK] * 5, [((4, 8 * own, units), half)])(both, *blocks)
    both = swap(both, "y").reshape(4, 4, 2, own, units)
    sides = [((D // 2, units), half)] * 2
    kept, given, bend, back = local(curve_first, [BLOCK] * 5, [*sides, square, square])(
        both, slopes, curves, tangent, rows
    )
    first = sum_copies(kept, given)

    lin, along = local(turn, [BLOCK] * 4, [((4, 4 * own, units), half), square])(
        rows, first, slopes, tangent
    )
    (stage,) = local(down, [BLOCK] * 5, [((4 * own, D), half)])(swap(lin, "y"), *blocks)
    stage = lax.all_gather(stage, "zh", axis=0)
    (moved,) = local(pull, [BLOCK] * 5, [((4, 4 * own, units), half)])(stage, *blocks)
    kept, given = local(curve_second, [BLOCK] * 6, sides)(
        swap(moved, "y"), slopes, bend, tangent, along, rows
    )
    second = sum_copies(kept, given)

    (terms,) = local(score, [BLOCK] * 5, [((16, 8, 128), full)])(
        rows, second, tangent, along, back
    )
    owned = jnp.sum(swap(terms, ("y", "zh"))).reshape(1)
    vector = (1.0 + rest * keep) * query_grad - (
        rest * first.astype(full) + second.astype(full)
    ) / TOKENS
    return (vector, -owned / (own * math.sqrt(D * FF)))


def solution(mesh):
    fine = Mesh(mesh.devices.reshape(SIZES), AXES)
    fsdp, everyone = AXES[:2], AXES
    placed = (
        P(everyone, None),
        P(everyone, None),
        P(None, everyone, None, None),
        P(everyone),
        P(everyone),
        P(None, fsdp),
        P(fsdp, None),
        P(None, fsdp),
    )
    return jax.shard_map(
        shards,
        mesh=fine,
        in_specs=placed,
        out_specs=(P(None, fsdp), P(everyone)),
        check_vma=False,
    )
```

time: 277 us -> 260 us (0.939)
  blocking collectives: 226 us -> 193 us
  starting transfers between devices: 17.1 us -> 36.7 us
  Pallas kernels: 0 us -> 6.22 us
  matrix products: 6.17 us -> 0 us
  other arithmetic: 5.58 us -> 2.1 us
  waiting for transfers between devices: 12 us -> 14.9 us
    all_to_all x11, blocking collectives: 174 us -> 141 us  [swap(): return lax.all_to_all(blocks, axes, 0, 0)]
    ppermute x2 -> x5, starting transfers between devices: 13.6 us -> 29.6 us  [the longest x2 18.7 us: sum_copies(): taken = lax.ppermute(given, 'c', [(0, 1), (1, 0)])]
    pallas_call x0 -> x10, Pallas kernels: none -> 6.22 us  [the longest x1 1.13 us: shards(): local(attend, [SCALARS, SCALARS, BLOCK, BLOCK, BLOCK], [((4, own, D), hal...]
    dot_general x14 -> x0, matrix products: 6.17 us -> none  [the longest x1 1.17 us: attend(): jnp.einsum('zilf,zgf->zilg', probe_length, lookup_length, preferred_eleme...]
    all_to_all x1, starting transfers between devices: 3.52 us -> 7.07 us  [swap(): return lax.all_to_all(blocks, axes, 0, 0)]
    all_to_all x1, waiting for transfers between devices: 9.7 us -> 12.7 us  [swap(): return lax.all_to_all(blocks, axes, 0, 0)]
  transfers between devices with their start and end apart: 3 -> 6, of which waited for: 3 -> 3; matrix products, arithmetic and copies ran while one was open for 0% -> 0% of each run, Pallas kernels for 0% -> 0%
where the time goes in v4:
time: 260 us; the launch traced here: 259 us
  blocking collectives  193 us (74%)
  starting transfers between devices  36.7 us (14%)
  waiting for transfers between devices  14.9 us (6%)
  Pallas kernels  6.22 us (2%)
  between operations  3.36 us (1%)
  local copies, waits for them, and re-layouts  2.62 us (1%)
    all_to_all x11, blocking collectives, swap(): return lax.all_to_all(blocks, axes, 0, 0)  141 us
    all_gather x1, blocking collectives, shards(): stage = lax.all_gather(stage, 'zh', axis=0)  26.9 us
    ppermute x2, starting transfers between devices, sum_copies(): taken = lax.ppermute(given, 'c', [(0, 1), (1, 0)])  18.7 us
    all_gather x1, blocking collectives, shards(): both = lax.all_gather(both, 'zh', axis=0).reshape(8 * own, D)  17.1 us
    all_to_all x1, waiting for transfers between devices, swap(): return lax.all_to_all(blocks, axes, 0, 0)  12.7 us
    ppermute x3, starting transfers between devices, shards(): lax.ppermute(w_down, 'y', [((i + shift) % 4, i) for i in range(4)])  10.9 us
    all_gather x2, blocking collectives, sum_copies(): return lax.all_gather(rows, 'c', axis=0, tiled=True)  8.25 us
    all_to_all x1, starting transfers between devices, swap(): return lax.all_to_all(blocks, axes, 0, 0)  7.07 us
  transfers between devices with their start and end apart: 6, of which 3 were waited for; matrix products, arithmetic and copies ran while one was open for 0% of the time, Pallas kernels for 0%

profile of v4, /device:TPU:1, one launch (start us, length us, event | category | flops | bytes accessed | tf_op | source)
XLA Modules:
  0.0 259.4 jit_solution(15509144679718913790)
XLA Ops:
  0.6 5.7 %collective-permute-start.1 = (bf16[256,1024]{1,0:T(8,128)(2,1)}, bf16[256,1024]{1,0:T(8,128)(2,1)S(1)}, u32[]{:S(2)}, u32[]{:S(2)}) collective-permute-start(bf16[256,1024]{1,0:T(8,128)(2,1)} %refs_0_.3), channel_id=1, source_target_pairs={{64,0},{96,32},{0,64},{32,96},{65,1},{97,33},{1,65},{33,97},{66,2}... | collective-permute-start | bytes 1572872 | tf_op jit(solution)/shard_map/ppermute | solution.py:212
  6.3 2.7 %collective-permute-start = (bf16[256,1024]{1,0:T(8,128)(2,1)}, bf16[256,1024]{1,0:T(8,128)(2,1)S(1)}, u32[]{:S(2)}, u32[]{:S(2)}) collective-permute-start(bf16[256,1024]{1,0:T(8,128)(2,1)} %refs_0_.3), channel_id=1, source_target_pairs={{32,0},{64,32},{96,64},{0,96},{33,1},{65,33},{97,65},{1,97},{34,2}... | collective-permute-start | bytes 1572872 | tf_op jit(solution)/shard_map/ppermute | solution.py:212
  9.0 2.6 %collective-permute-start.2 = (bf16[256,1024]{1,0:T(8,128)(2,1)}, bf16[256,1024]{1,0:T(8,128)(2,1)S(1)}, u32[]{:S(2)}, u32[]{:S(2)}) collective-permute-start(bf16[256,1024]{1,0:T(8,128)(2,1)} %refs_0_.3), channel_id=1, source_target_pairs={{96,0},{0,32},{32,64},{64,96},{97,1},{1,33},{33,65},{65,97},{98,2}... | collective-permute-start | bytes 1572872 | tf_op jit(solution)/shard_map/ppermute | solution.py:212
  12.3 0.9 copy-done.8
  13.2 0.8 copy-done.13
  14.0 0.8 copy-done.14
  14.7 1.1 shard_map.95
  15.9 26.9 %all_to_all.60 = bf16[4,16,1024]{2,1,0:T(8,128)(2,1)S(1)} all-to-all(bf16[4,16,1024]{2,1,0:T(8,128)(2,1)S(1)} %get-tuple-element.22), channel_id=1, replica_groups=mesh['zh'=4,'y'=4,'x'=4,'zl'=4,'c'=2] {'zh'}, dimensions={0} | all-to-all | bytes 262144 | tf_op jit(solution)/shard_map/all_to_all | solution.py:183
  42.9 10.1 %all_to_all.61 = bf16[4,4,16,1024]{3,2,1,0:T(8,128)(2,1)S(1)} all-to-all(bf16[4,4,16,1024]{3,2,1,0:T(8,128)(2,1)S(1)} %broadcast_in_dim.6), channel_id=1, replica_groups=mesh['zh'=4,'y'=4,'x'=4,'zl'=4,'c'=2] {'y'}, dimensions={0} | all-to-all | bytes 1048576 | tf_op jit(solution)/shard_map/all_to_all | solution.py:183
  53.6 8.0 %all_to_all.62.lin_ref = bf16[4,4,2,16,256]{4,3,2,1,0:T(8,128)(2,1)S(1)} all-to-all(bf16[4,4,2,16,256]{4,3,2,1,0:T(8,128)(2,1)S(1)} %get-tuple-element.24), channel_id=1, replica_groups=mesh['zh'=4,'y'=4,'x'=4,'zl'=4,'c'=2] {'y'}, dimensions={0} | all-to-all | bytes 524288 | tf_op jit(solution)/shard_map/all_to_all | solution.py:183
  62.1 18.3 %all_to_all.63 = bf16[4,2,16,1024]{3,2,1,0:T(8,128)(2,1)S(1)} all-to-all(bf16[4,2,16,1024]{3,2,1,0:T(8,128)(2,1)S(1)} %bitcast.27), channel_id=1, replica_groups=mesh['zh'=4,'y'=4,'x'=4,'zl'=4,'c'=2] {'zh'}, dimensions={0} | all-to-all | bytes 524288 | tf_op jit(solution)/shard_map/all_to_all | solution.py:183
  80.5 17.1 %all-gather = bf16[8,16,1024]{2,1,0:T(8,128)(2,1)S(1)} all-gather(bf16[2,16,1024]{2,1,0:T(8,128)(2,1)S(1)} %pad_maximum_fusion), channel_id=2, replica_groups=mesh['zh'=4,'y'=4,'x'=4,'zl'=4,'c'=2] {'zh'}, dimensions={0}, use_global_device_ids=true | all-gather | bytes 327680 | tf_op jit(solution)/shard_map/all_gather | solution.py:227
  97.6 0.8 shard_map.98
  98.5 8.2 %all_to_all.64 = bf16[4,128,256]{2,1,0:T(8,128)(2,1)S(1)} all-to-all(bf16[4,128,256]{2,1,0:T(8,128)(2,1)S(1)} %shard_map.98), channel_id=1, replica_groups=mesh['zh'=4,'y'=4,'x'=4,'zl'=4,'c'=2] {'y'}, dimensions={0} | all-to-all | bytes 524288 | tf_op jit(solution)/shard_map/all_to_all | solution.py:183
  107.1 12.9 %collective-permute-start.3 = (bf16[512,256]{1,0:T(8,128)(2,1)S(1)}, bf16[512,256]{1,0:T(8,128)(2,1)S(1)}, u32[]{:S(2)}, u32[]{:S(2)}) collective-permute-start(bf16[512,256]{1,0:T(8,128)(2,1)S(1)} %get-tuple-element.33), channel_id=1, source_target_pairs={{0,1},{1,0},{2,3},{3,2},{4,5},{5,4},{6,7},{7,6},{8,9},{9,8},{10,11... | collective-permute-start | bytes 786440 | tf_op jit(solution)/shard_map/ppermute | solution.py:196
  120.0 1.1 collective-permute-done.3
  121.2 15.8 %all_to_all.65 = bf16[16,32,256]{2,1,0:T(8,128)(2,1)S(1)} all-to-all(bf16[16,32,256]{2,1,0:T(8,128)(2,1)S(1)} %bitcast.29), channel_id=1, replica_groups=mesh['zh'=4,'y'=4,'x'=4,'zl'=4,'c'=2] {'x','zl'}, dimensions={0} | all-to-all | bytes 524288 | tf_op jit(solution)/shard_map/all_to_all | solution.py:183
  137.1 13.1 %all_to_all.66 = bf16[16,32,256]{2,1,0:T(8,128)(2,1)S(1)} all-to-all(bf16[16,32,256]{2,1,0:T(8,128)(2,1)S(1)} %broadcast_in_dim.7), channel_id=1, replica_groups=mesh['zh'=4,'y'=4,'x'=4,'zl'=4,'c'=2] {'x','zl'}, dimensions={0} | all-to-all | bytes 524288 | tf_op jit(solution)/shard_map/all_to_all | solution.py:183
  150.2 4.2 %all_gather.20.first_ref = bf16[1024,256]{1,0:T(8,128)(2,1)S(1)} all-gather(bf16[512,256]{1,0:T(8,128)(2,1)S(1)} %bitcast.31), channel_id=1, replica_groups=mesh['zh'=4,'y'=4,'x'=4,'zl'=4,'c'=2] {'c'}, dimensions={0}, use_global_device_ids=true | all-gather | bytes 786432 | tf_op jit(solution)/shard_map/all_gather | solution.py:200
  154.7 7.2 %all_to_all.67.lin_ref = bf16[4,64,256]{2,1,0:T(8,128)(2,1)S(1)} all-to-all(bf16[4,64,256]{2,1,0:T(8,128)(2,1)S(1)} %get-tuple-element.34), channel_id=1, replica_groups=mesh['zh'=4,'y'=4,'x'=4,'zl'=4,'c'=2] {'y'}, dimensions={0} | all-to-all | bytes 262144 | tf_op jit(solution)/shard_map/all_to_all | solution.py:183
  162.4 26.9 %all-gather.1 = bf16[256,1024]{1,0:T(8,128)(2,1)S(1)} all-gather(bf16[64,1024]{1,0:T(8,128)(2,1)S(1)} %shard_map.101), channel_id=3, replica_groups=mesh['zh'=4,'y'=4,'x'=4,'zl'=4,'c'=2] {'zh'}, dimensions={0}, use_global_device_ids=true | all-gather | bytes 655360 | tf_op jit(solution)/shard_map/all_gather | solution.py:240
  189.3 0.8 shard_map.102
  190.1 7.5 %all_to_all.68.moved_ref = bf16[4,64,256]{2,1,0:T(8,128)(2,1)S(1)} all-to-all(bf16[4,64,256]{2,1,0:T(8,128)(2,1)S(1)} %shard_map.102), channel_id=1, replica_groups=mesh['zh'=4,'y'=4,'x'=4,'zl'=4,'c'=2] {'y'}, dimensions={0} | all-to-all | bytes 262144 | tf_op jit(solution)/shard_map/all_to_all | solution.py:183
  198.0 5.8 %collective-permute-start.4 = (bf16[512,256]{1,0:T(8,128)(2,1)S(1)}, bf16[512,256]{1,0:T(8,128)(2,1)S(1)}, u32[]{:S(2)}, u32[]{:S(2)}) collective-permute-start(bf16[512,256]{1,0:T(8,128)(2,1)S(1)} %get-tuple-element.38), channel_id=1, source_target_pairs={{0,1},{1,0},{2,3},{3,2},{4,5},{5,4},{6,7},{7,6},{8,9},{9,8},{10,11... | collective-permute-start | bytes 786440 | tf_op jit(solution)/shard_map/ppermute | solution.py:196
  203.9 1.1 collective-permute-done.4
  205.1 12.6 %all_to_all.69 = bf16[16,32,256]{2,1,0:T(8,128)(2,1)S(1)} all-to-all(bf16[16,32,256]{2,1,0:T(8,128)(2,1)S(1)} %bitcast.30), channel_id=1, replica_groups=mesh['zh'=4,'y'=4,'x'=4,'zl'=4,'c'=2] {'x','zl'}, dimensions={0} | all-to-all | bytes 524288 | tf_op jit(solution)/shard_map/all_to_all | solution.py:183
  217.7 13.3 %all_to_all.70 = bf16[16,32,256]{2,1,0:T(8,128)(2,1)S(1)} all-to-all(bf16[16,32,256]{2,1,0:T(8,128)(2,1)S(1)} %broadcast_in_dim.8), channel_id=1, replica_groups=mesh['zh'=4,'y'=4,'x'=4,'zl'=4,'c'=2] {'x','zl'}, dimensions={0} | all-to-all | bytes 524288 | tf_op jit(solution)/shard_map/all_to_all | solution.py:183
  231.0 4.1 %all_gather.23.second_ref = bf16[1024,256]{1,0:T(8,128)(2,1)S(1)} all-gather(bf16[512,256]{1,0:T(8,128)(2,1)S(1)} %bitcast.32), channel_id=1, replica_groups=mesh['zh'=4,'y'=4,'x'=4,'zl'=4,'c'=2] {'c'}, dimensions={0}, use_global_device_ids=true | all-gather | bytes 786432 | tf_op jit(solution)/shard_map/all_gather | solution.py:200
  235.1 0.9 shard_map.104
  236.1 7.1 %all-to-all-start.11 = ((f32[16,8,128]{2,1,0:T(8,128)}), f32[16,8,128]{2,1,0:T(8,128)S(1)}, u32[]{:S(2)}, u32[]{:S(2)}) async-start(f32[16,8,128]{2,1,0:T(8,128)} %shard_map.104), calls=%async_computation.11 | async-start | bytes 131072 | tf_op jit(solution)/shard_map/all_to_all | solution.py:183
  243.1 1.2 multiply_subtract_fusion
  244.4 12.7 %all-to-all-done.11 = f32[16,8,128]{2,1,0:T(8,128)S(1)} async-done(((f32[16,8,128]{2,1,0:T(8,128)}), f32[16,8,128]{2,1,0:T(8,128)S(1)}, u32[]{:S(2)}, u32[]{:S(2)}) %all-to-all-start.11) | async-done | bytes 65568 | tf_op jit(solution)/shard_map/all_to_all | solution.py:183
  (50 shorter events, 3.6 us)
Async XLA Ops:
  0.6 11.6 %copy-start.15 = (s32[16]{0:T(128)S(1)}, s32[16]{0:T(128)}, u32[]{:S(2)}) copy-start(s32[16]{0:T(128)} %mask_ref.1) | copy-start | bytes 196
  0.6 42.2 %collective-permute-start.1 = (bf16[256,1024]{1,0:T(8,128)(2,1)}, bf16[256,1024]{1,0:T(8,128)(2,1)S(1)}, u32[]{:S(2)}, u32[]{:S(2)}) collective-permute-start(bf16[256,1024]{1,0:T(8,128)(2,1)} %refs_0_.3), channel_id=1, source_target_pairs={{64,0},{96,32},{0,64},{32,96},{65,1},{97,33},{1,65},{33,97},{66,2}... | collective-permute-start | bytes 1572872 | tf_op jit(solution)/shard_map/ppermute | solution.py:212
  6.3 36.5 %collective-permute-start = (bf16[256,1024]{1,0:T(8,128)(2,1)}, bf16[256,1024]{1,0:T(8,128)(2,1)S(1)}, u32[]{:S(2)}, u32[]{:S(2)}) collective-permute-start(bf16[256,1024]{1,0:T(8,128)(2,1)} %refs_0_.3), channel_id=1, source_target_pairs={{32,0},{64,32},{96,64},{0,96},{33,1},{65,33},{97,65},{1,97},{34,2}... | collective-permute-start | bytes 1572872 | tf_op jit(solution)/shard_map/ppermute | solution.py:212
  9.0 33.8 %collective-permute-start.2 = (bf16[256,1024]{1,0:T(8,128)(2,1)}, bf16[256,1024]{1,0:T(8,128)(2,1)S(1)}, u32[]{:S(2)}, u32[]{:S(2)}) collective-permute-start(bf16[256,1024]{1,0:T(8,128)(2,1)} %refs_0_.3), channel_id=1, source_target_pairs={{96,0},{0,32},{32,64},{64,96},{97,1},{1,33},{33,65},{65,97},{98,2}... | collective-permute-start | bytes 1572872 | tf_op jit(solution)/shard_map/ppermute | solution.py:212
  12.3 1.0 copy-start.8
  13.2 0.8 copy-start.13
  14.0 0.8 copy-start.14
  15.9 37.2 %copy-start.1 = (f32[1024,256]{1,0:T(8,128)S(1)}, f32[1024,256]{1,0:T(8,128)}, u32[]{:S(2)}) copy-start(f32[1024,256]{1,0:T(8,128)} %query_ref.1) | copy-start | bytes 3145732
  42.9 10.1 %copy-start.7 = (bf16[1024,256]{1,0:T(8,128)(2,1)S(1)}, bf16[1024,256]{1,0:T(8,128)(2,1)}, u32[]{:S(2)}) copy-start(bf16[1024,256]{1,0:T(8,128)(2,1)} %up_ref.1) | copy-start | bytes 1572868
  53.5 53.1 %copy-start.3 = (f32[256,256]{1,0:T(8,128)}, f32[256,256]{1,0:T(8,128)S(1)}, u32[]{:S(2)}) copy-start(f32[256,256]{1,0:T(8,128)S(1)} %get-tuple-element.29.slopes_ref) | copy-start | bytes 786436
  53.6 8.1 %copy-start = (bf16[256,1024]{1,0:T(8,128)(2,1)S(1)}, bf16[256,1024]{1,0:T(8,128)(2,1)}, u32[]{:S(2)}) copy-start(bf16[256,1024]{1,0:T(8,128)(2,1)} %refs_0_.3) | copy-start | bytes 1572868
  107.1 14.1 %copy-start.9 = (f32[256,256]{1,0:T(8,128)}, f32[256,256]{1,0:T(8,128)S(1)}, u32[]{:S(2)}) copy-start(f32[256,256]{1,0:T(8,128)S(1)} %get-tuple-element.35.bend_ref) | copy-start | bytes 786436
  107.1 14.1 %copy-start.11 = (f32[256,256]{1,0:T(8,128)}, f32[256,256]{1,0:T(8,128)S(1)}, u32[]{:S(2)}) copy-start(f32[256,256]{1,0:T(8,128)S(1)} %get-tuple-element.39.back_ref) | copy-start | bytes 786436
  107.1 14.0 %collective-permute-start.3 = (bf16[512,256]{1,0:T(8,128)(2,1)S(1)}, bf16[512,256]{1,0:T(8,128)(2,1)S(1)}, u32[]{:S(2)}, u32[]{:S(2)}) collective-permute-start(bf16[512,256]{1,0:T(8,128)(2,1)S(1)} %get-tuple-element.33), channel_id=1, source_target_pairs={{0,1},{1,0},{2,3},{3,2},{4,5},{5,4},{6,7},{7,6},{8,9},{9,8},{10,11... | collective-permute-start | bytes 786440 | tf_op jit(solution)/shard_map/ppermute | solution.py:196
  150.2 4.2 %copy-start.4 = (f32[256,256]{1,0:T(8,128)S(1)}, f32[256,256]{1,0:T(8,128)}, u32[]{:S(2)}) copy-start(f32[256,256]{1,0:T(8,128)} %copy-done.3) | copy-start | bytes 786436
  154.7 42.9 %copy-start.5 = (f32[256,256]{1,0:T(8,128)}, f32[256,256]{1,0:T(8,128)S(1)}, u32[]{:S(2)}) copy-start(f32[256,256]{1,0:T(8,128)S(1)} %get-tuple-element.36.along_ref) | copy-start | bytes 786436
  190.1 7.5 %copy-start.10 = (f32[256,256]{1,0:T(8,128)S(1)}, f32[256,256]{1,0:T(8,128)}, u32[]{:S(2)}) copy-start(f32[256,256]{1,0:T(8,128)} %copy-done.9) | copy-start | bytes 786436
  198.0 7.0 %collective-permute-start.4 = (bf16[512,256]{1,0:T(8,128)(2,1)S(1)}, bf16[512,256]{1,0:T(8,128)(2,1)S(1)}, u32[]{:S(2)}, u32[]{:S(2)}) collective-permute-start(bf16[512,256]{1,0:T(8,128)(2,1)S(1)} %get-tuple-element.38), channel_id=1, source_target_pairs={{0,1},{1,0},{2,3},{3,2},{4,5},{5,4},{6,7},{7,6},{8,9},{9,8},{10,11... | collective-permute-start | bytes 786440 | tf_op jit(solution)/shard_map/ppermute | solution.py:196
  231.0 4.1 %copy-start.6 = (f32[256,256]{1,0:T(8,128)S(1)}, f32[256,256]{1,0:T(8,128)}, u32[]{:S(2)}) copy-start(f32[256,256]{1,0:T(8,128)} %copy-done.5) | copy-start | bytes 786436
  231.0 4.1 %copy-start.12 = (f32[256,256]{1,0:T(8,128)S(1)}, f32[256,256]{1,0:T(8,128)}, u32[]{:S(2)}) copy-start(f32[256,256]{1,0:T(8,128)} %copy-done.11) | copy-start | bytes 786436
  235.1 8.0 %copy-start.2 = (f32[1024,256]{1,0:T(8,128)S(1)}, f32[1024,256]{1,0:T(8,128)}, u32[]{:S(2)}) copy-start(f32[1024,256]{1,0:T(8,128)} %query_ref.1) | copy-start | bytes 3145732
  236.1 21.0 %all-to-all-start.11 = ((f32[16,8,128]{2,1,0:T(8,128)}), f32[16,8,128]{2,1,0:T(8,128)S(1)}, u32[]{:S(2)}, u32[]{:S(2)}) async-start(f32[16,8,128]{2,1,0:T(8,128)} %shard_map.104), calls=%async_computation.11 | async-start | bytes 131072 | tf_op jit(solution)/shard_map/all_to_all | solution.py:183

commit v5 on v4

--- a/solution.py
+++ b/solution.py
@@ -28,11 +28,15 @@
 BLOCK = pl.BlockSpec(memory_space=pltpu.VMEM)
 
 
-def local(kernel, specs, outs):
+FAR = pl.BlockSpec(memory_space=pltpu.HBM)
+
+
+def local(kernel, specs, outs, out_specs=None, scratch=()):
     return pl.pallas_call(
         kernel,
         in_specs=specs,
-        out_specs=[BLOCK] * len(outs),
+        out_specs=out_specs or [BLOCK] * len(outs),
+        scratch_shapes=scratch,
         out_shape=[jax.ShapeDtypeStruct(shape, dtype) for shape, dtype in outs],
         compiler_params=pltpu.CompilerParams(vmem_limit_bytes=24 * 2**20),
     )
@@ -54,7 +58,20 @@
     )
 
 
-def attend(flow_ref, mask_ref, noise_ref, action_ref, kv_ref, sent_ref, resid_ref):
+def attend(
+    flow_ref, mask_ref, noise_far, action_far, kv_far, sent_ref, resid_ref,
+    noise_ref, action_ref, kv_ref, sems,
+):
+    copies = [
+        pltpu.make_async_copy(far, near, sems.at[i])
+        for i, (far, near) in enumerate(
+            ((kv_far, kv_ref), (noise_far, noise_ref), (action_far, action_ref))
+        )
+    ]
+    for copy in copies:
+        copy.start()
+    for copy in copies:
+        copy.wait()
     acts, width = noise_ref.shape
     span = kv_ref.shape[3]
     heads = width // span
@@ -171,12 +188,26 @@
     halves(rows_ref, second, kept_ref, given_ref)
 
 
-def score(rows_ref, second_ref, tangent_ref, along_ref, back_ref, terms_ref):
+def score(
+    rows_ref, second_ref, tangent_ref, along_ref, back_ref, first_ref, query_ref,
+    terms_ref, vector_far, vector_ref, sem,
+):
+    first = first_ref[...].astype(jnp.float32)
+    second = second_ref[...].astype(jnp.float32)
+    vector_ref[...] = (1.0 + rest * keep) * query_ref[...] - (rest * first + second) / TOKENS
+    copy = pltpu.make_async_copy(vector_ref, vector_far, sem)
+    copy.start()
     along = nn(rows_ref[...], second_ref[...]) / TOKENS
     projected = (1.0 + rest * keep) * tangent_ref[...] - rest * along_ref[...] - along
-    terms = (projected * back_ref[...]).reshape(16, 2, 8, 256)
-    terms = terms[:, 0] + terms[:, 1]
-    terms_ref[...] = terms[:, :, :128] + terms[:, :, 128:]
+    terms = (projected * back_ref[...]).reshape(16, 16, 256)
+    terms = jnp.sum(terms[:, :, :128] + terms[:, :, 128:], 1, keepdims=True)
+    terms_ref[...] = terms
+    copy.wait()
+
+
+def finish(terms_ref, score_ref):
+    acts = TOKENS // 512
+    score_ref[0] = -jnp.sum(terms_ref[...]) / (acts * math.sqrt(D * FF))
 
 
 def swap(blocks, axes):
@@ -213,8 +244,14 @@
 
     sent, resid = local(
         attend,
-        [SCALARS, SCALARS, BLOCK, BLOCK, BLOCK],
+        [SCALARS, SCALARS, FAR, FAR, FAR],
         [((4, own, D), half), ((own, D), full)],
+        scratch=[
+            pltpu.VMEM(noise_embed.shape, half),
+            pltpu.VMEM(action_embed.shape, half),
+            pltpu.VMEM(prefix_kv.shape, half),
+            pltpu.SemaphoreType.DMA((3,)),
+        ],
     )(flow_step, action_mask, noise_embed, action_embed, prefix_kv)
     stage, blocks = lax.optimization_barrier((swap(sent, "zh"), blocks))
     rows = collect(stage, "y", 4).reshape(tokens, D)
@@ -224,7 +261,7 @@
     (stage,) = local(down, [BLOCK] * 5, [((8 * own, D), half)])(swap(lin, "y"), *blocks)
     both = total(swap(stage.reshape(4, 2, own, D), "zh"))
     both = jnp.stack([(resid + both[0]).astype(half), both[1].astype(half)])
-    both = lax.all_gather(both, "zh", axis=0).reshape(8 * own, D)
+    both = collect(both, "zh", 4).reshape(8 * own, D)
     (both,) = local(pull, [BLOCK] * 5, [((4, 8 * own, units), half)])(both, *blocks)
     both = swap(both, "y").reshape(4, 4, 2, own, units)
     sides = [((D // 2, units), half)] * 2
@@ -244,14 +281,15 @@
     )
     second = sum_copies(kept, given)
 
-    (terms,) = local(score, [BLOCK] * 5, [((16, 8, 128), full)])(
-        rows, second, tangent, along, back
-    )
-    owned = jnp.sum(swap(terms, ("y", "zh"))).reshape(1)
-    vector = (1.0 + rest * keep) * query_grad - (
-        rest * first.astype(full) + second.astype(full)
-    ) / TOKENS
-    return (vector, -owned / (own * math.sqrt(D * FF)))
+    terms, vector = local(
+        score,
+        [BLOCK] * 7,
+        [((16, 1, 128), full), (query_grad.shape, full)],
+        [BLOCK, FAR],
+        [pltpu.VMEM(query_grad.shape, full), pltpu.SemaphoreType.DMA],
+    )(rows, second, tangent, along, back, first, query_grad)
+    (owned,) = local(finish, [BLOCK], [((1,), full)], [SCALARS])(swap(terms, ("y", "zh")))
+    return (vector, owned)
 
 
 def solution(mesh):

time: 260 us -> 257 us (0.988)
  blocking collectives: 193 us -> 214 us
  waiting for transfers between devices: 14.9 us -> 2.29 us
  starting transfers between devices: 36.7 us -> 27.1 us
    all_to_all x11 -> x13, blocking collectives: 141 us -> 179 us  [swap(): return lax.all_to_all(blocks, axes, 0, 0)]
    all_gather x1 -> x0, blocking collectives: 17.1 us -> none  [shards(): both = lax.all_gather(both, 'zh', axis=0).reshape(8 * own, D)]
    all_to_all x1 -> x0, waiting for transfers between devices: 12.7 us -> none  [swap(): return lax.all_to_all(blocks, axes, 0, 0)]
    all_to_all x1 -> x0, starting transfers between devices: 7.07 us -> none  [swap(): return lax.all_to_all(blocks, axes, 0, 0)]
  transfers between devices with their start and end apart: 6 -> 5, of which waited for: 3 -> 2; matrix products, arithmetic and copies ran while one was open for 0% -> 0% of each run, Pallas kernels for 0% -> 0%
where the time goes in v5:
time: 257 us; the launch traced here: 256 us
  blocking collectives  214 us (83%)
  starting transfers between devices  27.1 us (11%)
  Pallas kernels  7.77 us (3%)
  local copies, waits for them, and re-layouts  2.64 us (1%)
    all_to_all x13, blocking collectives, swap(): return lax.all_to_all(blocks, axes, 0, 0)  179 us
    all_gather x1, blocking collectives, shards(): stage = lax.all_gather(stage, 'zh', axis=0)  27.1 us
    ppermute x2, starting transfers between devices, sum_copies(): taken = lax.ppermute(given, 'c', [(0, 1), (1, 0)])  16.2 us
    ppermute x3, starting transfers between devices, shards(): lax.ppermute(w_down, 'y', [((i + shift) % 4, i) for i in range(4)])  10.9 us
    all_gather x2, blocking collectives, sum_copies(): return lax.all_gather(rows, 'c', axis=0, tiled=True)  8.25 us
  transfers between devices with their start and end apart: 5, of which 2 were waited for; matrix products, arithmetic and copies ran while one was open for 0% of the time, Pallas kernels for 0%

profile of v5, /device:TPU:1, one launch (start us, length us, event | category | flops | bytes accessed | tf_op | source)
XLA Modules:
  0.0 256.0 jit_solution(2187527897211031879)
XLA Ops:
  0.6 5.7 %collective-permute-start.1 = (bf16[256,1024]{1,0:T(8,128)(2,1)}, bf16[256,1024]{1,0:T(8,128)(2,1)S(1)}, u32[]{:S(2)}, u32[]{:S(2)}) collective-permute-start(bf16[256,1024]{1,0:T(8,128)(2,1)} %refs_0_.3), channel_id=1, source_target_pairs={{64,0},{96,32},{0,64},{32,96},{65,1},{97,33},{1,65},{33,97},{66,2}... | collective-permute-start | bytes 1572872 | tf_op jit(solution)/shard_map/ppermute | solution.py:243
  6.3 2.7 %collective-permute-start = (bf16[256,1024]{1,0:T(8,128)(2,1)}, bf16[256,1024]{1,0:T(8,128)(2,1)S(1)}, u32[]{:S(2)}, u32[]{:S(2)}) collective-permute-start(bf16[256,1024]{1,0:T(8,128)(2,1)} %refs_0_.3), channel_id=1, source_target_pairs={{32,0},{64,32},{96,64},{0,96},{33,1},{65,33},{97,65},{1,97},{34,2}... | collective-permute-start | bytes 1572872 | tf_op jit(solution)/shard_map/ppermute | solution.py:243
  9.0 2.6 %collective-permute-start.2 = (bf16[256,1024]{1,0:T(8,128)(2,1)}, bf16[256,1024]{1,0:T(8,128)(2,1)S(1)}, u32[]{:S(2)}, u32[]{:S(2)}) collective-permute-start(bf16[256,1024]{1,0:T(8,128)(2,1)} %refs_0_.3), channel_id=1, source_target_pairs={{96,0},{0,32},{32,64},{64,96},{97,1},{1,33},{33,65},{65,97},{98,2}... | collective-permute-start | bytes 1572872 | tf_op jit(solution)/shard_map/ppermute | solution.py:243
  12.3 0.9 copy-done.8
  13.2 0.8 copy-done.13
  14.0 0.8 copy-done.14
  14.7 1.3 shard_map.95
  16.0 26.9 %all_to_all.65 = bf16[4,16,1024]{2,1,0:T(8,128)(2,1)S(1)} all-to-all(bf16[4,16,1024]{2,1,0:T(8,128)(2,1)S(1)} %get-tuple-element.23), channel_id=1, replica_groups=mesh['zh'=4,'y'=4,'x'=4,'zl'=4,'c'=2] {'zh'}, dimensions={0} | all-to-all | bytes 262144 | tf_op jit(solution)/shard_map/all_to_all | solution.py:214
  43.0 10.1 %all_to_all.66 = bf16[4,4,16,1024]{3,2,1,0:T(8,128)(2,1)S(1)} all-to-all(bf16[4,4,16,1024]{3,2,1,0:T(8,128)(2,1)S(1)} %broadcast_in_dim.8), channel_id=1, replica_groups=mesh['zh'=4,'y'=4,'x'=4,'zl'=4,'c'=2] {'y'}, dimensions={0} | all-to-all | bytes 1048576 | tf_op jit(solution)/shard_map/all_to_all | solution.py:214
  53.2 0.5 shard_map.96
  53.7 8.0 %all_to_all.67.lin_ref = bf16[4,4,2,16,256]{4,3,2,1,0:T(8,128)(2,1)S(1)} all-to-all(bf16[4,4,2,16,256]{4,3,2,1,0:T(8,128)(2,1)S(1)} %get-tuple-element.26), channel_id=1, replica_groups=mesh['zh'=4,'y'=4,'x'=4,'zl'=4,'c'=2] {'y'}, dimensions={0} | all-to-all | bytes 524288 | tf_op jit(solution)/shard_map/all_to_all | solution.py:214
  62.2 18.3 %all_to_all.68 = bf16[4,2,16,1024]{3,2,1,0:T(8,128)(2,1)S(1)} all-to-all(bf16[4,2,16,1024]{3,2,1,0:T(8,128)(2,1)S(1)} %bitcast.25), channel_id=1, replica_groups=mesh['zh'=4,'y'=4,'x'=4,'zl'=4,'c'=2] {'zh'}, dimensions={0} | all-to-all | bytes 524288 | tf_op jit(solution)/shard_map/all_to_all | solution.py:214
  80.7 18.4 %all_to_all.69 = bf16[4,2,16,1024]{3,2,1,0:T(8,128)(2,1)S(1)} all-to-all(bf16[4,2,16,1024]{3,2,1,0:T(8,128)(2,1)S(1)} %broadcast_in_dim.9), channel_id=1, replica_groups=mesh['zh'=4,'y'=4,'x'=4,'zl'=4,'c'=2] {'zh'}, dimensions={0} | all-to-all | bytes 524288 | tf_op jit(solution)/shard_map/all_to_all | solution.py:214
  99.1 0.8 shard_map.98
  99.9 7.9 %all_to_all.70 = bf16[4,128,256]{2,1,0:T(8,128)(2,1)S(1)} all-to-all(bf16[4,128,256]{2,1,0:T(8,128)(2,1)S(1)} %shard_map.98), channel_id=1, replica_groups=mesh['zh'=4,'y'=4,'x'=4,'zl'=4,'c'=2] {'y'}, dimensions={0} | all-to-all | bytes 524288 | tf_op jit(solution)/shard_map/all_to_all | solution.py:214
  108.3 12.1 %collective-permute-start.3 = (bf16[512,256]{1,0:T(8,128)(2,1)S(1)}, bf16[512,256]{1,0:T(8,128)(2,1)S(1)}, u32[]{:S(2)}, u32[]{:S(2)}) collective-permute-start(bf16[512,256]{1,0:T(8,128)(2,1)S(1)} %get-tuple-element.35), channel_id=1, source_target_pairs={{0,1},{1,0},{2,3},{3,2},{4,5},{5,4},{6,7},{7,6},{8,9},{9,8},{10,11... | collective-permute-start | bytes 786440 | tf_op jit(solution)/shard_map/ppermute | solution.py:227
  120.4 1.1 collective-permute-done.3
  121.6 15.1 %all_to_all.71 = bf16[16,32,256]{2,1,0:T(8,128)(2,1)S(1)} all-to-all(bf16[16,32,256]{2,1,0:T(8,128)(2,1)S(1)} %bitcast.28), channel_id=1, replica_groups=mesh['zh'=4,'y'=4,'x'=4,'zl'=4,'c'=2] {'x','zl'}, dimensions={0} | all-to-all | bytes 524288 | tf_op jit(solution)/shard_map/all_to_all | solution.py:214
  136.8 13.1 %all_to_all.72 = bf16[16,32,256]{2,1,0:T(8,128)(2,1)S(1)} all-to-all(bf16[16,32,256]{2,1,0:T(8,128)(2,1)S(1)} %broadcast_in_dim.10), channel_id=1, replica_groups=mesh['zh'=4,'y'=4,'x'=4,'zl'=4,'c'=2] {'x','zl'}, dimensions={0} | all-to-all | bytes 524288 | tf_op jit(solution)/shard_map/all_to_all | solution.py:214
  149.9 4.2 %all_gather.12.first_ref = bf16[1024,256]{1,0:T(8,128)(2,1)S(1)} all-gather(bf16[512,256]{1,0:T(8,128)(2,1)S(1)} %bitcast.30), channel_id=1, replica_groups=mesh['zh'=4,'y'=4,'x'=4,'zl'=4,'c'=2] {'c'}, dimensions={0}, use_global_device_ids=true | all-gather | bytes 786432 | tf_op jit(solution)/shard_map/all_gather | solution.py:231
  154.4 7.2 %all_to_all.73.lin_ref = bf16[4,64,256]{2,1,0:T(8,128)(2,1)S(1)} all-to-all(bf16[4,64,256]{2,1,0:T(8,128)(2,1)S(1)} %get-tuple-element.36), channel_id=1, replica_groups=mesh['zh'=4,'y'=4,'x'=4,'zl'=4,'c'=2] {'y'}, dimensions={0} | all-to-all | bytes 262144 | tf_op jit(solution)/shard_map/all_to_all | solution.py:214
  162.1 27.1 %all-gather = bf16[256,1024]{1,0:T(8,128)(2,1)S(1)} all-gather(bf16[64,1024]{1,0:T(8,128)(2,1)S(1)} %shard_map.101), channel_id=2, replica_groups=mesh['zh'=4,'y'=4,'x'=4,'zl'=4,'c'=2] {'zh'}, dimensions={0}, use_global_device_ids=true | all-gather | bytes 655360 | tf_op jit(solution)/shard_map/all_gather | solution.py:277
  189.2 0.8 shard_map.102
  190.0 7.3 %all_to_all.74.moved_ref = bf16[4,64,256]{2,1,0:T(8,128)(2,1)S(1)} all-to-all(bf16[4,64,256]{2,1,0:T(8,128)(2,1)S(1)} %shard_map.102), channel_id=1, replica_groups=mesh['zh'=4,'y'=4,'x'=4,'zl'=4,'c'=2] {'y'}, dimensions={0} | all-to-all | bytes 262144 | tf_op jit(solution)/shard_map/all_to_all | solution.py:214
  197.7 4.1 %collective-permute-start.4 = (bf16[512,256]{1,0:T(8,128)(2,1)S(1)}, bf16[512,256]{1,0:T(8,128)(2,1)S(1)}, u32[]{:S(2)}, u32[]{:S(2)}) collective-permute-start(bf16[512,256]{1,0:T(8,128)(2,1)S(1)} %get-tuple-element.40), channel_id=1, source_target_pairs={{0,1},{1,0},{2,3},{3,2},{4,5},{5,4},{6,7},{7,6},{8,9},{9,8},{10,11... | collective-permute-start | bytes 786440 | tf_op jit(solution)/shard_map/ppermute | solution.py:227
  201.8 1.1 collective-permute-done.4
  203.0 12.6 %all_to_all.75 = bf16[16,32,256]{2,1,0:T(8,128)(2,1)S(1)} all-to-all(bf16[16,32,256]{2,1,0:T(8,128)(2,1)S(1)} %bitcast.29), channel_id=1, replica_groups=mesh['zh'=4,'y'=4,'x'=4,'zl'=4,'c'=2] {'x','zl'}, dimensions={0} | all-to-all | bytes 524288 | tf_op jit(solution)/shard_map/all_to_all | solution.py:214
  215.7 13.4 %all_to_all.76 = bf16[16,32,256]{2,1,0:T(8,128)(2,1)S(1)} all-to-all(bf16[16,32,256]{2,1,0:T(8,128)(2,1)S(1)} %broadcast_in_dim.11), channel_id=1, replica_groups=mesh['zh'=4,'y'=4,'x'=4,'zl'=4,'c'=2] {'x','zl'}, dimensions={0} | all-to-all | bytes 524288 | tf_op jit(solution)/shard_map/all_to_all | solution.py:214
  229.1 4.1 %all_gather.15.second_ref = bf16[1024,256]{1,0:T(8,128)(2,1)S(1)} all-gather(bf16[512,256]{1,0:T(8,128)(2,1)S(1)} %bitcast.31), channel_id=1, replica_groups=mesh['zh'=4,'y'=4,'x'=4,'zl'=4,'c'=2] {'c'}, dimensions={0}, use_global_device_ids=true | all-gather | bytes 786432 | tf_op jit(solution)/shard_map/all_gather | solution.py:231
  233.2 1.7 shard_map.104
  234.9 20.5 %all_to_all.77.terms_ref = f32[16,1,128]{2,1,0:T(1,128)S(1)} all-to-all(f32[16,1,128]{2,1,0:T(1,128)S(1)} %get-tuple-element.43), channel_id=1, replica_groups=mesh['zh'=4,'y'=4,'x'=4,'zl'=4,'c'=2] {'y','zh'}, dimensions={0} | all-to-all | bytes 16384 | tf_op jit(solution)/shard_map/all_to_all | solution.py:214
  255.4 0.7 shard_map.105
  (49 shorter events, 2.5 us)
Async XLA Ops:
  0.6 11.6 %copy-start.15 = (s32[16]{0:T(128)S(1)}, s32[16]{0:T(128)}, u32[]{:S(2)}) copy-start(s32[16]{0:T(128)} %mask_ref.1) | copy-start | bytes 196
  0.6 42.3 %collective-permute-start.1 = (bf16[256,1024]{1,0:T(8,128)(2,1)}, bf16[256,1024]{1,0:T(8,128)(2,1)S(1)}, u32[]{:S(2)}, u32[]{:S(2)}) collective-permute-start(bf16[256,1024]{1,0:T(8,128)(2,1)} %refs_0_.3), channel_id=1, source_target_pairs={{64,0},{96,32},{0,64},{32,96},{65,1},{97,33},{1,65},{33,97},{66,2}... | collective-permute-start | bytes 1572872 | tf_op jit(solution)/shard_map/ppermute | solution.py:243
  6.3 36.7 %collective-permute-start = (bf16[256,1024]{1,0:T(8,128)(2,1)}, bf16[256,1024]{1,0:T(8,128)(2,1)S(1)}, u32[]{:S(2)}, u32[]{:S(2)}) collective-permute-start(bf16[256,1024]{1,0:T(8,128)(2,1)} %refs_0_.3), channel_id=1, source_target_pairs={{32,0},{64,32},{96,64},{0,96},{33,1},{65,33},{97,65},{1,97},{34,2}... | collective-permute-start | bytes 1572872 | tf_op jit(solution)/shard_map/ppermute | solution.py:243
  9.0 34.0 %collective-permute-start.2 = (bf16[256,1024]{1,0:T(8,128)(2,1)}, bf16[256,1024]{1,0:T(8,128)(2,1)S(1)}, u32[]{:S(2)}, u32[]{:S(2)}) collective-permute-start(bf16[256,1024]{1,0:T(8,128)(2,1)} %refs_0_.3), channel_id=1, source_target_pairs={{96,0},{0,32},{32,64},{64,96},{97,1},{1,33},{33,65},{65,97},{98,2}... | collective-permute-start | bytes 1572872 | tf_op jit(solution)/shard_map/ppermute | solution.py:243
  12.3 1.0 copy-start.8
  13.2 0.8 copy-start.13
  14.0 0.8 copy-start.14
  16.0 37.2 %copy-start.1 = (f32[1024,256]{1,0:T(8,128)S(1)}, f32[1024,256]{1,0:T(8,128)}, u32[]{:S(2)}) copy-start(f32[1024,256]{1,0:T(8,128)} %query_ref.3) | copy-start | bytes 3145732
  43.0 10.1 %copy-start.7 = (bf16[1024,256]{1,0:T(8,128)(2,1)S(1)}, bf16[1024,256]{1,0:T(8,128)(2,1)}, u32[]{:S(2)}) copy-start(bf16[1024,256]{1,0:T(8,128)(2,1)} %up_ref.1) | copy-start | bytes 1572868
  53.7 54.1 %copy-start.3 = (f32[256,256]{1,0:T(8,128)}, f32[256,256]{1,0:T(8,128)S(1)}, u32[]{:S(2)}) copy-start(f32[256,256]{1,0:T(8,128)S(1)} %get-tuple-element.31.slopes_ref) | copy-start | bytes 786436
  53.7 8.1 %copy-start = (bf16[256,1024]{1,0:T(8,128)(2,1)S(1)}, bf16[256,1024]{1,0:T(8,128)(2,1)}, u32[]{:S(2)}) copy-start(bf16[256,1024]{1,0:T(8,128)(2,1)} %refs_0_.3) | copy-start | bytes 1572868
  108.2 13.3 %copy-start.9 = (f32[256,256]{1,0:T(8,128)}, f32[256,256]{1,0:T(8,128)S(1)}, u32[]{:S(2)}) copy-start(f32[256,256]{1,0:T(8,128)S(1)} %get-tuple-element.37.bend_ref) | copy-start | bytes 786436
  108.2 13.3 %copy-start.11 = (f32[256,256]{1,0:T(8,128)}, f32[256,256]{1,0:T(8,128)S(1)}, u32[]{:S(2)}) copy-start(f32[256,256]{1,0:T(8,128)S(1)} %get-tuple-element.41.back_ref) | copy-start | bytes 786436
  108.3 13.2 %collective-permute-start.3 = (bf16[512,256]{1,0:T(8,128)(2,1)S(1)}, bf16[512,256]{1,0:T(8,128)(2,1)S(1)}, u32[]{:S(2)}, u32[]{:S(2)}) collective-permute-start(bf16[512,256]{1,0:T(8,128)(2,1)S(1)} %get-tuple-element.35), channel_id=1, source_target_pairs={{0,1},{1,0},{2,3},{3,2},{4,5},{5,4},{6,7},{7,6},{8,9},{9,8},{10,11... | collective-permute-start | bytes 786440 | tf_op jit(solution)/shard_map/ppermute | solution.py:227
  149.9 4.2 %copy-start.4 = (f32[256,256]{1,0:T(8,128)S(1)}, f32[256,256]{1,0:T(8,128)}, u32[]{:S(2)}) copy-start(f32[256,256]{1,0:T(8,128)} %copy-done.3) | copy-start | bytes 786436
  154.4 42.9 %copy-start.5 = (f32[256,256]{1,0:T(8,128)}, f32[256,256]{1,0:T(8,128)S(1)}, u32[]{:S(2)}) copy-start(f32[256,256]{1,0:T(8,128)S(1)} %get-tuple-element.38.along_ref) | copy-start | bytes 786436
  189.9 7.4 %copy-start.10 = (f32[256,256]{1,0:T(8,128)S(1)}, f32[256,256]{1,0:T(8,128)}, u32[]{:S(2)}) copy-start(f32[256,256]{1,0:T(8,128)} %copy-done.9) | copy-start | bytes 786436
  197.7 5.2 %collective-permute-start.4 = (bf16[512,256]{1,0:T(8,128)(2,1)S(1)}, bf16[512,256]{1,0:T(8,128)(2,1)S(1)}, u32[]{:S(2)}, u32[]{:S(2)}) collective-permute-start(bf16[512,256]{1,0:T(8,128)(2,1)S(1)} %get-tuple-element.40), channel_id=1, source_target_pairs={{0,1},{1,0},{2,3},{3,2},{4,5},{5,4},{6,7},{7,6},{8,9},{9,8},{10,11... | collective-permute-start | bytes 786440 | tf_op jit(solution)/shard_map/ppermute | solution.py:227
  215.6 17.6 %copy-start.2 = (f32[1024,256]{1,0:T(8,128)S(1)}, f32[1024,256]{1,0:T(8,128)}, u32[]{:S(2)}) copy-start(f32[1024,256]{1,0:T(8,128)} %query_ref.3) | copy-start | bytes 3145732
  229.1 4.1 %copy-start.6 = (f32[256,256]{1,0:T(8,128)S(1)}, f32[256,256]{1,0:T(8,128)}, u32[]{:S(2)}) copy-start(f32[256,256]{1,0:T(8,128)} %copy-done.5) | copy-start | bytes 786436
  229.1 4.1 %copy-start.12 = (f32[256,256]{1,0:T(8,128)S(1)}, f32[256,256]{1,0:T(8,128)}, u32[]{:S(2)}) copy-start(f32[256,256]{1,0:T(8,128)} %copy-done.11) | copy-start | bytes 786436

commit v6 on v5

--- a/solution.py
+++ b/solution.py
@@ -210,6 +210,11 @@
     score_ref[0] = -jnp.sum(terms_ref[...]) / (acts * math.sqrt(D * FF))
 
 
+def join(kept_ref, both_ref, pair_ref):
+    taken = both_ref[1 - lax.axis_index("c")].astype(jnp.float32)
+    pair_ref[...] = (kept_ref[...].astype(jnp.float32) + taken).astype(jnp.bfloat16)
+
+
 def swap(blocks, axes):
     return lax.all_to_all(blocks, axes, 0, 0)
 
@@ -224,8 +229,8 @@
 
 def sum_copies(kept, given):
     half, columns = kept.shape
-    taken = lax.ppermute(given, "c", [(0, 1), (1, 0)])
-    pair = (kept.astype(jnp.float32) + taken.astype(jnp.float32)).astype(jnp.bfloat16)
+    both = lax.all_gather(given, "c", axis=0)
+    (pair,) = local(join, [BLOCK] * 2, [(kept.shape, kept.dtype)])(kept, both)
     rows = total(swap(pair.reshape(16, half // 16, columns), GRID))
     rows = collect(rows.astype(jnp.bfloat16), GRID, 16).reshape(half, columns)
     return lax.all_gather(rows, "c", axis=0, tiled=True)

time: 257 us -> 255 us (level)
  starting transfers between devices: 27.1 us -> 10.9 us
  blocking collectives: 214 us -> 230 us
    all_gather x0 -> x2, blocking collectives: none -> 16.3 us  [sum_copies(): both = lax.all_gather(given, 'c', axis=0)]
    ppermute x2 -> x0, starting transfers between devices: 16.2 us -> none  [sum_copies(): taken = lax.ppermute(given, 'c', [(0, 1), (1, 0)])]
  transfers between devices with their start and end apart: 5 -> 3, of which waited for: 2 -> 0; matrix products, arithmetic and copies ran while one was open for 0% -> 0% of each run, Pallas kernels for 0% -> 0%
where the time goes in v6:
time: 255 us; the launch traced here: 254 us
  blocking collectives  230 us (90%)
  starting transfers between devices  10.9 us (4%)
  Pallas kernels  7.9 us (3%)
  local copies, waits for them, and re-layouts  3.32 us (1%)
    all_to_all x13, blocking collectives, swap(): return lax.all_to_all(blocks, axes, 0, 0)  179 us
    all_gather x1, blocking collectives, shards(): stage = lax.all_gather(stage, 'zh', axis=0)  26.7 us
    all_gather x2, blocking collectives, sum_copies(): both = lax.all_gather(given, 'c', axis=0)  16.3 us
    ppermute x3, starting transfers between devices, shards(): lax.ppermute(w_down, 'y', [((i + shift) % 4, i) for i in range(4)])  10.9 us
    all_gather x2, blocking collectives, sum_copies(): return lax.all_gather(rows, 'c', axis=0, tiled=True)  8.25 us
  transfers between devices with their start and end apart: 3, of which 0 were waited for; matrix products, arithmetic and copies ran while one was open for 0% of the time, Pallas kernels for 0%

profile of v6, /device:TPU:1, one launch (start us, length us, event | category | flops | bytes accessed | tf_op | source)
XLA Modules:
  0.0 254.1 jit_solution(7720522046536684655)
XLA Ops:
  0.6 5.7 %collective-permute-start.1 = (bf16[256,1024]{1,0:T(8,128)(2,1)}, bf16[256,1024]{1,0:T(8,128)(2,1)S(1)}, u32[]{:S(2)}, u32[]{:S(2)}) collective-permute-start(bf16[256,1024]{1,0:T(8,128)(2,1)} %refs_0_.3), channel_id=1, source_target_pairs={{64,0},{96,32},{0,64},{32,96},{65,1},{97,33},{1,65},{33,97},{66,2}... | collective-permute-start | bytes 1572872 | tf_op jit(solution)/shard_map/ppermute | solution.py:248
  6.3 2.7 %collective-permute-start = (bf16[256,1024]{1,0:T(8,128)(2,1)}, bf16[256,1024]{1,0:T(8,128)(2,1)S(1)}, u32[]{:S(2)}, u32[]{:S(2)}) collective-permute-start(bf16[256,1024]{1,0:T(8,128)(2,1)} %refs_0_.3), channel_id=1, source_target_pairs={{32,0},{64,32},{96,64},{0,96},{33,1},{65,33},{97,65},{1,97},{34,2}... | collective-permute-start | bytes 1572872 | tf_op jit(solution)/shard_map/ppermute | solution.py:248
  9.0 2.6 %collective-permute-start.2 = (bf16[256,1024]{1,0:T(8,128)(2,1)}, bf16[256,1024]{1,0:T(8,128)(2,1)S(1)}, u32[]{:S(2)}, u32[]{:S(2)}) collective-permute-start(bf16[256,1024]{1,0:T(8,128)(2,1)} %refs_0_.3), channel_id=1, source_target_pairs={{96,0},{0,32},{32,64},{64,96},{97,1},{1,33},{33,65},{65,97},{98,2}... | collective-permute-start | bytes 1572872 | tf_op jit(solution)/shard_map/ppermute | solution.py:248
  12.3 0.9 copy-done.8
  13.2 0.8 copy-done.13
  14.0 0.8 copy-done.14
  14.7 1.3 shard_map.95
  16.0 26.9 %all_to_all.65 = bf16[4,16,1024]{2,1,0:T(8,128)(2,1)S(1)} all-to-all(bf16[4,16,1024]{2,1,0:T(8,128)(2,1)S(1)} %get-tuple-element.23), channel_id=1, replica_groups=mesh['zh'=4,'y'=4,'x'=4,'zl'=4,'c'=2] {'zh'}, dimensions={0} | all-to-all | bytes 262144 | tf_op jit(solution)/shard_map/all_to_all | solution.py:219
  43.0 10.1 %all_to_all.66 = bf16[4,4,16,1024]{3,2,1,0:T(8,128)(2,1)S(1)} all-to-all(bf16[4,4,16,1024]{3,2,1,0:T(8,128)(2,1)S(1)} %broadcast_in_dim.8), channel_id=1, replica_groups=mesh['zh'=4,'y'=4,'x'=4,'zl'=4,'c'=2] {'y'}, dimensions={0} | all-to-all | bytes 1048576 | tf_op jit(solution)/shard_map/all_to_all | solution.py:219
  53.2 0.5 shard_map.96
  53.7 8.0 %all_to_all.67.lin_ref = bf16[4,4,2,16,256]{4,3,2,1,0:T(8,128)(2,1)S(1)} all-to-all(bf16[4,4,2,16,256]{4,3,2,1,0:T(8,128)(2,1)S(1)} %get-tuple-element.26), channel_id=1, replica_groups=mesh['zh'=4,'y'=4,'x'=4,'zl'=4,'c'=2] {'y'}, dimensions={0} | all-to-all | bytes 524288 | tf_op jit(solution)/shard_map/all_to_all | solution.py:219
  62.2 18.3 %all_to_all.68 = bf16[4,2,16,1024]{3,2,1,0:T(8,128)(2,1)S(1)} all-to-all(bf16[4,2,16,1024]{3,2,1,0:T(8,128)(2,1)S(1)} %bitcast.29), channel_id=1, replica_groups=mesh['zh'=4,'y'=4,'x'=4,'zl'=4,'c'=2] {'zh'}, dimensions={0} | all-to-all | bytes 524288 | tf_op jit(solution)/shard_map/all_to_all | solution.py:219
  80.7 18.4 %all_to_all.69 = bf16[4,2,16,1024]{3,2,1,0:T(8,128)(2,1)S(1)} all-to-all(bf16[4,2,16,1024]{3,2,1,0:T(8,128)(2,1)S(1)} %broadcast_in_dim.9), channel_id=1, replica_groups=mesh['zh'=4,'y'=4,'x'=4,'zl'=4,'c'=2] {'zh'}, dimensions={0} | all-to-all | bytes 524288 | tf_op jit(solution)/shard_map/all_to_all | solution.py:219
  99.1 0.8 shard_map.98
  99.9 7.9 %all_to_all.70 = bf16[4,128,256]{2,1,0:T(8,128)(2,1)S(1)} all-to-all(bf16[4,128,256]{2,1,0:T(8,128)(2,1)S(1)} %shard_map.98), channel_id=1, replica_groups=mesh['zh'=4,'y'=4,'x'=4,'zl'=4,'c'=2] {'y'}, dimensions={0} | all-to-all | bytes 524288 | tf_op jit(solution)/shard_map/all_to_all | solution.py:219
  108.2 0.7 copy-done.9
  108.9 12.0 %all-gather = bf16[1024,256]{1,0:T(8,128)(2,1)S(1)} all-gather(bf16[512,256]{1,0:T(8,128)(2,1)S(1)} %get-tuple-element.35), channel_id=2, replica_groups=mesh['zh'=4,'y'=4,'x'=4,'zl'=4,'c'=2] {'c'}, dimensions={0}, use_global_device_ids=true | all-gather | bytes 786432 | tf_op jit(solution)/shard_map/all_gather | solution.py:232
  121.0 15.1 %all_to_all.71 = bf16[16,32,256]{2,1,0:T(8,128)(2,1)S(1)} all-to-all(bf16[16,32,256]{2,1,0:T(8,128)(2,1)S(1)} %bitcast.32), channel_id=1, replica_groups=mesh['zh'=4,'y'=4,'x'=4,'zl'=4,'c'=2] {'x','zl'}, dimensions={0} | all-to-all | bytes 524288 | tf_op jit(solution)/shard_map/all_to_all | solution.py:219
  136.2 13.1 %all_to_all.72 = bf16[16,32,256]{2,1,0:T(8,128)(2,1)S(1)} all-to-all(bf16[16,32,256]{2,1,0:T(8,128)(2,1)S(1)} %broadcast_in_dim.10), channel_id=1, replica_groups=mesh['zh'=4,'y'=4,'x'=4,'zl'=4,'c'=2] {'x','zl'}, dimensions={0} | all-to-all | bytes 524288 | tf_op jit(solution)/shard_map/all_to_all | solution.py:219
  149.3 4.2 %all_gather.26.first_ref = bf16[1024,256]{1,0:T(8,128)(2,1)S(1)} all-gather(bf16[512,256]{1,0:T(8,128)(2,1)S(1)} %bitcast.34), channel_id=1, replica_groups=mesh['zh'=4,'y'=4,'x'=4,'zl'=4,'c'=2] {'c'}, dimensions={0}, use_global_device_ids=true | all-gather | bytes 786432 | tf_op jit(solution)/shard_map/all_gather | solution.py:236
  153.8 7.2 %all_to_all.73.lin_ref = bf16[4,64,256]{2,1,0:T(8,128)(2,1)S(1)} all-to-all(bf16[4,64,256]{2,1,0:T(8,128)(2,1)S(1)} %get-tuple-element.36), channel_id=1, replica_groups=mesh['zh'=4,'y'=4,'x'=4,'zl'=4,'c'=2] {'y'}, dimensions={0} | all-to-all | bytes 262144 | tf_op jit(solution)/shard_map/all_to_all | solution.py:219
  161.0 0.5 shard_map.102
  161.5 26.7 %all-gather.1 = bf16[256,1024]{1,0:T(8,128)(2,1)S(1)} all-gather(bf16[64,1024]{1,0:T(8,128)(2,1)S(1)} %shard_map.102), channel_id=3, replica_groups=mesh['zh'=4,'y'=4,'x'=4,'zl'=4,'c'=2] {'zh'}, dimensions={0}, use_global_device_ids=true | all-gather | bytes 655360 | tf_op jit(solution)/shard_map/all_gather | solution.py:282
  188.2 0.8 shard_map.103
  189.0 7.3 %all_to_all.74.moved_ref = bf16[4,64,256]{2,1,0:T(8,128)(2,1)S(1)} all-to-all(bf16[4,64,256]{2,1,0:T(8,128)(2,1)S(1)} %shard_map.103), channel_id=1, replica_groups=mesh['zh'=4,'y'=4,'x'=4,'zl'=4,'c'=2] {'y'}, dimensions={0} | all-to-all | bytes 262144 | tf_op jit(solution)/shard_map/all_to_all | solution.py:219
  196.7 4.3 %all-gather.2 = bf16[1024,256]{1,0:T(8,128)(2,1)S(1)} all-gather(bf16[512,256]{1,0:T(8,128)(2,1)S(1)} %get-tuple-element.40), channel_id=4, replica_groups=mesh['zh'=4,'y'=4,'x'=4,'zl'=4,'c'=2] {'c'}, dimensions={0}, use_global_device_ids=true | all-gather | bytes 786432 | tf_op jit(solution)/shard_map/all_gather | solution.py:232
  201.1 12.6 %all_to_all.75 = bf16[16,32,256]{2,1,0:T(8,128)(2,1)S(1)} all-to-all(bf16[16,32,256]{2,1,0:T(8,128)(2,1)S(1)} %bitcast.33), channel_id=1, replica_groups=mesh['zh'=4,'y'=4,'x'=4,'zl'=4,'c'=2] {'x','zl'}, dimensions={0} | all-to-all | bytes 524288 | tf_op jit(solution)/shard_map/all_to_all | solution.py:219
  213.8 13.4 %all_to_all.76 = bf16[16,32,256]{2,1,0:T(8,128)(2,1)S(1)} all-to-all(bf16[16,32,256]{2,1,0:T(8,128)(2,1)S(1)} %broadcast_in_dim.11), channel_id=1, replica_groups=mesh['zh'=4,'y'=4,'x'=4,'zl'=4,'c'=2] {'x','zl'}, dimensions={0} | all-to-all | bytes 524288 | tf_op jit(solution)/shard_map/all_to_all | solution.py:219
  227.2 4.1 %all_gather.31.second_ref = bf16[1024,256]{1,0:T(8,128)(2,1)S(1)} all-gather(bf16[512,256]{1,0:T(8,128)(2,1)S(1)} %bitcast.35), channel_id=1, replica_groups=mesh['zh'=4,'y'=4,'x'=4,'zl'=4,'c'=2] {'c'}, dimensions={0}, use_global_device_ids=true | all-gather | bytes 786432 | tf_op jit(solution)/shard_map/all_gather | solution.py:236
  231.3 1.7 shard_map.106
  233.0 20.5 %all_to_all.77.terms_ref = f32[16,1,128]{2,1,0:T(1,128)S(1)} all-to-all(f32[16,1,128]{2,1,0:T(1,128)S(1)} %get-tuple-element.43), channel_id=1, replica_groups=mesh['zh'=4,'y'=4,'x'=4,'zl'=4,'c'=2] {'y','zh'}, dimensions={0} | all-to-all | bytes 16384 | tf_op jit(solution)/shard_map/all_to_all | solution.py:219
  253.5 0.7 shard_map.107
  (47 shorter events, 2.1 us)
Async XLA Ops:
  0.6 11.6 %copy-start.15 = (s32[16]{0:T(128)S(1)}, s32[16]{0:T(128)}, u32[]{:S(2)}) copy-start(s32[16]{0:T(128)} %mask_ref.1) | copy-start | bytes 196
  0.6 42.3 %collective-permute-start.1 = (bf16[256,1024]{1,0:T(8,128)(2,1)}, bf16[256,1024]{1,0:T(8,128)(2,1)S(1)}, u32[]{:S(2)}, u32[]{:S(2)}) collective-permute-start(bf16[256,1024]{1,0:T(8,128)(2,1)} %refs_0_.3), channel_id=1, source_target_pairs={{64,0},{96,32},{0,64},{32,96},{65,1},{97,33},{1,65},{33,97},{66,2}... | collective-permute-start | bytes 1572872 | tf_op jit(solution)/shard_map/ppermute | solution.py:248
  6.3 36.7 %collective-permute-start = (bf16[256,1024]{1,0:T(8,128)(2,1)}, bf16[256,1024]{1,0:T(8,128)(2,1)S(1)}, u32[]{:S(2)}, u32[]{:S(2)}) collective-permute-start(bf16[256,1024]{1,0:T(8,128)(2,1)} %refs_0_.3), channel_id=1, source_target_pairs={{32,0},{64,32},{96,64},{0,96},{33,1},{65,33},{97,65},{1,97},{34,2}... | collective-permute-start | bytes 1572872 | tf_op jit(solution)/shard_map/ppermute | solution.py:248
  9.0 34.0 %collective-permute-start.2 = (bf16[256,1024]{1,0:T(8,128)(2,1)}, bf16[256,1024]{1,0:T(8,128)(2,1)S(1)}, u32[]{:S(2)}, u32[]{:S(2)}) collective-permute-start(bf16[256,1024]{1,0:T(8,128)(2,1)} %refs_0_.3), channel_id=1, source_target_pairs={{96,0},{0,32},{32,64},{64,96},{97,1},{1,33},{33,65},{65,97},{98,2}... | collective-permute-start | bytes 1572872 | tf_op jit(solution)/shard_map/ppermute | solution.py:248
  12.3 1.0 copy-start.8
  13.2 0.8 copy-start.13
  14.0 0.8 copy-start.14
  16.0 37.2 %copy-start.1 = (f32[1024,256]{1,0:T(8,128)S(1)}, f32[1024,256]{1,0:T(8,128)}, u32[]{:S(2)}) copy-start(f32[1024,256]{1,0:T(8,128)} %query_ref.3) | copy-start | bytes 3145732
  43.0 10.1 %copy-start.7 = (bf16[1024,256]{1,0:T(8,128)(2,1)S(1)}, bf16[1024,256]{1,0:T(8,128)(2,1)}, u32[]{:S(2)}) copy-start(bf16[1024,256]{1,0:T(8,128)(2,1)} %up_ref.1) | copy-start | bytes 1572868
  53.7 54.1 %copy-start.3 = (f32[256,256]{1,0:T(8,128)}, f32[256,256]{1,0:T(8,128)S(1)}, u32[]{:S(2)}) copy-start(f32[256,256]{1,0:T(8,128)S(1)} %get-tuple-element.31.slopes_ref) | copy-start | bytes 786436
  53.7 8.1 %copy-start = (bf16[256,1024]{1,0:T(8,128)(2,1)S(1)}, bf16[256,1024]{1,0:T(8,128)(2,1)}, u32[]{:S(2)}) copy-start(bf16[256,1024]{1,0:T(8,128)(2,1)} %refs_0_.3) | copy-start | bytes 1572868
  108.2 0.7 copy-start.9
  108.9 12.0 %copy-start.11 = (f32[256,256]{1,0:T(8,128)}, f32[256,256]{1,0:T(8,128)S(1)}, u32[]{:S(2)}) copy-start(f32[256,256]{1,0:T(8,128)S(1)} %get-tuple-element.41.back_ref) | copy-start | bytes 786436
  149.3 4.2 %copy-start.4 = (f32[256,256]{1,0:T(8,128)S(1)}, f32[256,256]{1,0:T(8,128)}, u32[]{:S(2)}) copy-start(f32[256,256]{1,0:T(8,128)} %copy-done.3) | copy-start | bytes 786436
  153.8 42.5 %copy-start.5 = (f32[256,256]{1,0:T(8,128)}, f32[256,256]{1,0:T(8,128)S(1)}, u32[]{:S(2)}) copy-start(f32[256,256]{1,0:T(8,128)S(1)} %get-tuple-element.38.along_ref) | copy-start | bytes 786436
  189.0 7.4 %copy-start.10 = (f32[256,256]{1,0:T(8,128)S(1)}, f32[256,256]{1,0:T(8,128)}, u32[]{:S(2)}) copy-start(f32[256,256]{1,0:T(8,128)} %copy-done.9) | copy-start | bytes 786436
  213.7 17.6 %copy-start.2 = (f32[1024,256]{1,0:T(8,128)S(1)}, f32[1024,256]{1,0:T(8,128)}, u32[]{:S(2)}) copy-start(f32[1024,256]{1,0:T(8,128)} %query_ref.3) | copy-start | bytes 3145732
  227.2 4.1 %copy-start.6 = (f32[256,256]{1,0:T(8,128)S(1)}, f32[256,256]{1,0:T(8,128)}, u32[]{:S(2)}) copy-start(f32[256,256]{1,0:T(8,128)} %copy-done.5) | copy-start | bytes 786436
  227.2 4.1 %copy-start.12 = (f32[256,256]{1,0:T(8,128)S(1)}, f32[256,256]{1,0:T(8,128)}, u32[]{:S(2)}) copy-start(f32[256,256]{1,0:T(8,128)} %copy-done.11) | copy-start | bytes 786436

commit v7 on v6

--- a/solution.py
+++ b/solution.py
@@ -215,6 +215,15 @@
     pair_ref[...] = (kept_ref[...].astype(jnp.float32) + taken).astype(jnp.bfloat16)
 
 
+def spread(blocks_ref, copies_ref):
+    out = blocks_ref[0].astype(jnp.float32)
+    for i in range(1, blocks_ref.shape[0]):
+        out = out + blocks_ref[i].astype(jnp.float32)
+    out = out.astype(jnp.bfloat16)
+    for i in range(copies_ref.shape[0]):
+        copies_ref[i] = out
+
+
 def swap(blocks, axes):
     return lax.all_to_all(blocks, axes, 0, 0)
 
@@ -231,8 +240,9 @@
     half, columns = kept.shape
     both = lax.all_gather(given, "c", axis=0)
     (pair,) = local(join, [BLOCK] * 2, [(kept.shape, kept.dtype)])(kept, both)
-    rows = total(swap(pair.reshape(16, half // 16, columns), GRID))
-    rows = collect(rows.astype(jnp.bfloat16), GRID, 16).reshape(half, columns)
+    shape = (16, half // 16, columns)
+    (rows,) = local(spread, [BLOCK], [(shape, pair.dtype)])(swap(pair.reshape(shape), GRID))
+    rows = swap(rows, GRID).reshape(half, columns)
     return lax.all_gather(rows, "c", axis=0, tiled=True)
 
 

time: 255 us -> 253 us (level)
  transfers between devices with their start and end apart: 3 -> 3, of which waited for: 0 -> 0; matrix products, arithmetic and copies ran while one was open for 0% -> 0% of each run, Pallas kernels for 0% -> 1%
where the time goes in v7:
time: 253 us
  blocking collectives  229 us (91%)
  starting transfers between devices  10.9 us (4%)
  Pallas kernels  8.07 us (3%)
  local copies, waits for them, and re-layouts  2.56 us (1%)
    all_to_all x13, blocking collectives, swap(): return lax.all_to_all(blocks, axes, 0, 0)  179 us
    all_gather x1, blocking collectives, shards(): stage = lax.all_gather(stage, 'zh', axis=0)  26.6 us
    all_gather x2, blocking collectives, sum_copies(): both = lax.all_gather(given, 'c', axis=0)  16 us
    ppermute x3, starting transfers between devices, shards(): lax.ppermute(w_down, 'y', [((i + shift) % 4, i) for i in range(4)])  10.9 us
    all_gather x2, blocking collectives, sum_copies(): return lax.all_gather(rows, 'c', axis=0, tiled=True)  7.99 us
  transfers between devices with their start and end apart: 3, of which 0 were waited for; matrix products, arithmetic and copies ran while one was open for 0% of the time, Pallas kernels for 1%

profile of v7, /device:TPU:1, one launch (start us, length us, event | category | flops | bytes accessed | tf_op | source)
XLA Modules:
  0.0 252.6 jit_solution(5572574575150324306)
XLA Ops:
  0.6 5.7 %collective-permute-start.1 = (bf16[256,1024]{1,0:T(8,128)(2,1)}, bf16[256,1024]{1,0:T(8,128)(2,1)S(1)}, u32[]{:S(2)}, u32[]{:S(2)}) collective-permute-start(bf16[256,1024]{1,0:T(8,128)(2,1)} %refs_0_.3), channel_id=1, source_target_pairs={{64,0},{96,32},{0,64},{32,96},{65,1},{97,33},{1,65},{33,97},{66,2}... | collective-permute-start | bytes 1572872 | tf_op jit(solution)/shard_map/ppermute | solution.py:258
  6.3 2.7 %collective-permute-start = (bf16[256,1024]{1,0:T(8,128)(2,1)}, bf16[256,1024]{1,0:T(8,128)(2,1)S(1)}, u32[]{:S(2)}, u32[]{:S(2)}) collective-permute-start(bf16[256,1024]{1,0:T(8,128)(2,1)} %refs_0_.3), channel_id=1, source_target_pairs={{32,0},{64,32},{96,64},{0,96},{33,1},{65,33},{97,65},{1,97},{34,2}... | collective-permute-start | bytes 1572872 | tf_op jit(solution)/shard_map/ppermute | solution.py:258
  9.0 2.6 %collective-permute-start.2 = (bf16[256,1024]{1,0:T(8,128)(2,1)}, bf16[256,1024]{1,0:T(8,128)(2,1)S(1)}, u32[]{:S(2)}, u32[]{:S(2)}) collective-permute-start(bf16[256,1024]{1,0:T(8,128)(2,1)} %refs_0_.3), channel_id=1, source_target_pairs={{96,0},{0,32},{32,64},{64,96},{97,1},{1,33},{33,65},{65,97},{98,2}... | collective-permute-start | bytes 1572872 | tf_op jit(solution)/shard_map/ppermute | solution.py:258
  12.3 0.9 copy-done.3
  13.2 0.8 copy-done.4
  14.0 0.8 copy-done.5
  14.7 1.3 shard_map.95
  16.0 26.9 %all_to_all.65 = bf16[4,16,1024]{2,1,0:T(8,128)(2,1)S(1)} all-to-all(bf16[4,16,1024]{2,1,0:T(8,128)(2,1)S(1)} %get-tuple-element.23), channel_id=1, replica_groups=mesh['zh'=4,'y'=4,'x'=4,'zl'=4,'c'=2] {'zh'}, dimensions={0} | all-to-all | bytes 262144 | tf_op jit(solution)/shard_map/all_to_all | solution.py:228
  43.0 10.1 %all_to_all.66 = bf16[4,4,16,1024]{3,2,1,0:T(8,128)(2,1)S(1)} all-to-all(bf16[4,4,16,1024]{3,2,1,0:T(8,128)(2,1)S(1)} %broadcast_in_dim.4), channel_id=1, replica_groups=mesh['zh'=4,'y'=4,'x'=4,'zl'=4,'c'=2] {'y'}, dimensions={0} | all-to-all | bytes 1048576 | tf_op jit(solution)/shard_map/all_to_all | solution.py:228
  53.2 0.5 shard_map.96
  53.7 8.0 %all_to_all.67.lin_ref = bf16[4,4,2,16,256]{4,3,2,1,0:T(8,128)(2,1)S(1)} all-to-all(bf16[4,4,2,16,256]{4,3,2,1,0:T(8,128)(2,1)S(1)} %get-tuple-element.26), channel_id=1, replica_groups=mesh['zh'=4,'y'=4,'x'=4,'zl'=4,'c'=2] {'y'}, dimensions={0} | all-to-all | bytes 524288 | tf_op jit(solution)/shard_map/all_to_all | solution.py:228
  61.7 0.5 shard_map.97
  62.2 18.3 %all_to_all.68 = bf16[4,2,16,1024]{3,2,1,0:T(8,128)(2,1)S(1)} all-to-all(bf16[4,2,16,1024]{3,2,1,0:T(8,128)(2,1)S(1)} %bitcast.29), channel_id=1, replica_groups=mesh['zh'=4,'y'=4,'x'=4,'zl'=4,'c'=2] {'zh'}, dimensions={0} | all-to-all | bytes 524288 | tf_op jit(solution)/shard_map/all_to_all | solution.py:228
  80.7 18.4 %all_to_all.69 = bf16[4,2,16,1024]{3,2,1,0:T(8,128)(2,1)S(1)} all-to-all(bf16[4,2,16,1024]{3,2,1,0:T(8,128)(2,1)S(1)} %broadcast_in_dim.5), channel_id=1, replica_groups=mesh['zh'=4,'y'=4,'x'=4,'zl'=4,'c'=2] {'zh'}, dimensions={0} | all-to-all | bytes 524288 | tf_op jit(solution)/shard_map/all_to_all | solution.py:228
  99.1 0.8 shard_map.98
  99.9 7.9 %all_to_all.70 = bf16[4,128,256]{2,1,0:T(8,128)(2,1)S(1)} all-to-all(bf16[4,128,256]{2,1,0:T(8,128)(2,1)S(1)} %shard_map.98), channel_id=1, replica_groups=mesh['zh'=4,'y'=4,'x'=4,'zl'=4,'c'=2] {'y'}, dimensions={0} | all-to-all | bytes 524288 | tf_op jit(solution)/shard_map/all_to_all | solution.py:228
  108.3 12.0 %all-gather = bf16[1024,256]{1,0:T(8,128)(2,1)S(1)} all-gather(bf16[512,256]{1,0:T(8,128)(2,1)S(1)} %get-tuple-element.35), channel_id=2, replica_groups=mesh['zh'=4,'y'=4,'x'=4,'zl'=4,'c'=2] {'c'}, dimensions={0}, use_global_device_ids=true | all-gather | bytes 786432 | tf_op jit(solution)/shard_map/all_gather | solution.py:241
  120.3 15.2 %all_to_all.71.blocks_ref = bf16[16,32,256]{2,1,0:T(8,128)(2,1)S(1)} all-to-all(bf16[16,32,256]{2,1,0:T(8,128)(2,1)S(1)} %bitcast.32), channel_id=1, replica_groups=mesh['zh'=4,'y'=4,'x'=4,'zl'=4,'c'=2] {'x','zl'}, dimensions={0} | all-to-all | bytes 524288 | tf_op jit(solution)/shard_map/all_to_all | solution.py:228
  135.6 13.1 %all_to_all.72 = bf16[16,32,256]{2,1,0:T(8,128)(2,1)S(1)} all-to-all(bf16[16,32,256]{2,1,0:T(8,128)(2,1)S(1)} %shard_map.101), channel_id=1, replica_groups=mesh['zh'=4,'y'=4,'x'=4,'zl'=4,'c'=2] {'x','zl'}, dimensions={0} | all-to-all | bytes 524288 | tf_op jit(solution)/shard_map/all_to_all | solution.py:228
  148.7 4.0 %all_gather.26.first_ref = bf16[1024,256]{1,0:T(8,128)(2,1)S(1)} all-gather(bf16[512,256]{1,0:T(8,128)(2,1)S(1)} %bitcast.34), channel_id=1, replica_groups=mesh['zh'=4,'y'=4,'x'=4,'zl'=4,'c'=2] {'c'}, dimensions={0}, use_global_device_ids=true | all-gather | bytes 786432 | tf_op jit(solution)/shard_map/all_gather | solution.py:246
  153.0 7.2 %all_to_all.73.lin_ref = bf16[4,64,256]{2,1,0:T(8,128)(2,1)S(1)} all-to-all(bf16[4,64,256]{2,1,0:T(8,128)(2,1)S(1)} %get-tuple-element.36), channel_id=1, replica_groups=mesh['zh'=4,'y'=4,'x'=4,'zl'=4,'c'=2] {'y'}, dimensions={0} | all-to-all | bytes 262144 | tf_op jit(solution)/shard_map/all_to_all | solution.py:228
  160.3 0.5 shard_map.103
  160.8 26.6 %all-gather.1 = bf16[256,1024]{1,0:T(8,128)(2,1)S(1)} all-gather(bf16[64,1024]{1,0:T(8,128)(2,1)S(1)} %shard_map.103), channel_id=3, replica_groups=mesh['zh'=4,'y'=4,'x'=4,'zl'=4,'c'=2] {'zh'}, dimensions={0}, use_global_device_ids=true | all-gather | bytes 655360 | tf_op jit(solution)/shard_map/all_gather | solution.py:292
  187.4 0.8 shard_map.104
  188.1 7.2 %all_to_all.74.moved_ref = bf16[4,64,256]{2,1,0:T(8,128)(2,1)S(1)} all-to-all(bf16[4,64,256]{2,1,0:T(8,128)(2,1)S(1)} %shard_map.104), channel_id=1, replica_groups=mesh['zh'=4,'y'=4,'x'=4,'zl'=4,'c'=2] {'y'}, dimensions={0} | all-to-all | bytes 262144 | tf_op jit(solution)/shard_map/all_to_all | solution.py:228
  195.8 4.0 %all-gather.2 = bf16[1024,256]{1,0:T(8,128)(2,1)S(1)} all-gather(bf16[512,256]{1,0:T(8,128)(2,1)S(1)} %get-tuple-element.40), channel_id=4, replica_groups=mesh['zh'=4,'y'=4,'x'=4,'zl'=4,'c'=2] {'c'}, dimensions={0}, use_global_device_ids=true | all-gather | bytes 786432 | tf_op jit(solution)/shard_map/all_gather | solution.py:241
  199.9 12.6 %all_to_all.75.blocks_ref = bf16[16,32,256]{2,1,0:T(8,128)(2,1)S(1)} all-to-all(bf16[16,32,256]{2,1,0:T(8,128)(2,1)S(1)} %bitcast.33), channel_id=1, replica_groups=mesh['zh'=4,'y'=4,'x'=4,'zl'=4,'c'=2] {'x','zl'}, dimensions={0} | all-to-all | bytes 524288 | tf_op jit(solution)/shard_map/all_to_all | solution.py:228
  212.6 13.2 %all_to_all.76 = bf16[16,32,256]{2,1,0:T(8,128)(2,1)S(1)} all-to-all(bf16[16,32,256]{2,1,0:T(8,128)(2,1)S(1)} %shard_map.107), channel_id=1, replica_groups=mesh['zh'=4,'y'=4,'x'=4,'zl'=4,'c'=2] {'x','zl'}, dimensions={0} | all-to-all | bytes 524288 | tf_op jit(solution)/shard_map/all_to_all | solution.py:228
  225.8 4.0 %all_gather.31.second_ref = bf16[1024,256]{1,0:T(8,128)(2,1)S(1)} all-gather(bf16[512,256]{1,0:T(8,128)(2,1)S(1)} %bitcast.35), channel_id=1, replica_groups=mesh['zh'=4,'y'=4,'x'=4,'zl'=4,'c'=2] {'c'}, dimensions={0}, use_global_device_ids=true | all-gather | bytes 786432 | tf_op jit(solution)/shard_map/all_gather | solution.py:246
  229.7 1.7 shard_map.108
  231.4 20.5 %all_to_all.77.terms_ref = f32[16,1,128]{2,1,0:T(1,128)S(1)} all-to-all(f32[16,1,128]{2,1,0:T(1,128)S(1)} %get-tuple-element.43), channel_id=1, replica_groups=mesh['zh'=4,'y'=4,'x'=4,'zl'=4,'c'=2] {'y','zh'}, dimensions={0} | all-to-all | bytes 16384 | tf_op jit(solution)/shard_map/all_to_all | solution.py:228
  251.9 0.7 shard_map.109
  (27 shorter events, 1.6 us)
Async XLA Ops:
  0.6 11.6 %copy-start.6 = (s32[16]{0:T(128)S(1)}, s32[16]{0:T(128)}, u32[]{:S(2)}) copy-start(s32[16]{0:T(128)} %mask_ref.1) | copy-start | bytes 196
  0.6 42.3 %collective-permute-start.1 = (bf16[256,1024]{1,0:T(8,128)(2,1)}, bf16[256,1024]{1,0:T(8,128)(2,1)S(1)}, u32[]{:S(2)}, u32[]{:S(2)}) collective-permute-start(bf16[256,1024]{1,0:T(8,128)(2,1)} %refs_0_.3), channel_id=1, source_target_pairs={{64,0},{96,32},{0,64},{32,96},{65,1},{97,33},{1,65},{33,97},{66,2}... | collective-permute-start | bytes 1572872 | tf_op jit(solution)/shard_map/ppermute | solution.py:258
  6.3 36.7 %collective-permute-start = (bf16[256,1024]{1,0:T(8,128)(2,1)}, bf16[256,1024]{1,0:T(8,128)(2,1)S(1)}, u32[]{:S(2)}, u32[]{:S(2)}) collective-permute-start(bf16[256,1024]{1,0:T(8,128)(2,1)} %refs_0_.3), channel_id=1, source_target_pairs={{32,0},{64,32},{96,64},{0,96},{33,1},{65,33},{97,65},{1,97},{34,2}... | collective-permute-start | bytes 1572872 | tf_op jit(solution)/shard_map/ppermute | solution.py:258
  9.0 34.0 %collective-permute-start.2 = (bf16[256,1024]{1,0:T(8,128)(2,1)}, bf16[256,1024]{1,0:T(8,128)(2,1)S(1)}, u32[]{:S(2)}, u32[]{:S(2)}) collective-permute-start(bf16[256,1024]{1,0:T(8,128)(2,1)} %refs_0_.3), channel_id=1, source_target_pairs={{96,0},{0,32},{32,64},{64,96},{97,1},{1,33},{33,65},{65,97},{98,2}... | collective-permute-start | bytes 1572872 | tf_op jit(solution)/shard_map/ppermute | solution.py:258
  12.3 1.0 copy-start.3
  13.2 0.8 copy-start.4
  14.0 0.8 copy-start.5
  16.0 37.2 %copy-start.1 = (f32[1024,256]{1,0:T(8,128)S(1)}, f32[1024,256]{1,0:T(8,128)}, u32[]{:S(2)}) copy-start(f32[1024,256]{1,0:T(8,128)} %query_ref.3) | copy-start | bytes 3145732
  43.0 10.1 %copy-start.2 = (bf16[1024,256]{1,0:T(8,128)(2,1)S(1)}, bf16[1024,256]{1,0:T(8,128)(2,1)}, u32[]{:S(2)}) copy-start(bf16[1024,256]{1,0:T(8,128)(2,1)} %up_ref.1) | copy-start | bytes 1572868
  53.7 8.1 %copy-start = (bf16[256,1024]{1,0:T(8,128)(2,1)S(1)}, bf16[256,1024]{1,0:T(8,128)(2,1)}, u32[]{:S(2)}) copy-start(bf16[256,1024]{1,0:T(8,128)(2,1)} %refs_0_.3) | copy-start | bytes 1572868

commit v8 on v7

--- a/solution.py
+++ b/solution.py
@@ -224,16 +224,23 @@
         copies_ref[i] = out
 
 
+def settle(blocks_ref, resid_ref, copies_ref):
+    out = blocks_ref[0].astype(jnp.float32)
+    for i in range(1, blocks_ref.shape[0]):
+        out = out + blocks_ref[i].astype(jnp.float32)
+    err = (resid_ref[...] + out[0]).astype(jnp.bfloat16)
+    moved = out[1].astype(jnp.bfloat16)
+    for i in range(copies_ref.shape[0]):
+        copies_ref[i, 0] = err
+        copies_ref[i, 1] = moved
+
+
 def swap(blocks, axes):
     return lax.all_to_all(blocks, axes, 0, 0)
 
 
 def collect(block, axes, members):
     return swap(jnp.broadcast_to(block[None], (members, *block.shape)), axes)
-
-
-def total(blocks):
-    return jnp.sum(blocks.astype(jnp.float32), 0)
 
 
 def sum_copies(kept, given):
@@ -274,9 +281,9 @@
         forward, [BLOCK] * 3, [((4, 4, 2, own, units), half), square, square, square]
     )(rows, w_up, query_grad)
     (stage,) = local(down, [BLOCK] * 5, [((8 * own, D), half)])(swap(lin, "y"), *blocks)
-    both = total(swap(stage.reshape(4, 2, own, D), "zh"))
-    both = jnp.stack([(resid + both[0]).astype(half), both[1].astype(half)])
-    both = collect(both, "zh", 4).reshape(8 * own, D)
+    both = swap(stage.reshape(4, 2, own, D), "zh")
+    (both,) = local(settle, [BLOCK] * 2, [(both.shape, half)])(both, resid)
+    both = swap(both, "zh").reshape(8 * own, D)
     (both,) = local(pull, [BLOCK] * 5, [((4, 8 * own, units), half)])(both, *blocks)
     both = swap(both, "y").reshape(4, 4, 2, own, units)
     sides = [((D // 2, units), half)] * 2

time: 253 us -> 253 us (level)
  no operation moved by 1% of the time
where the time goes in v8:
time: 253 us; the launch traced here: 252 us
  blocking collectives  229 us (91%)
  starting transfers between devices  10.9 us (4%)
  Pallas kernels  8.1 us (3%)
    all_to_all x13, blocking collectives, swap(): return lax.all_to_all(blocks, axes, 0, 0)  179 us
    all_gather x1, blocking collectives, shards(): stage = lax.all_gather(stage, 'zh', axis=0)  26.6 us
    all_gather x2, blocking collectives, sum_copies(): both = lax.all_gather(given, 'c', axis=0)  16 us
    ppermute x3, starting transfers between devices, shards(): lax.ppermute(w_down, 'y', [((i + shift) % 4, i) for i in range(4)])  10.9 us
    all_gather x2, blocking collectives, sum_copies(): return lax.all_gather(rows, 'c', axis=0, tiled=True)  7.99 us
  transfers between devices with their start and end apart: 3, of which 0 were waited for; matrix products, arithmetic and copies ran while one was open for 0% of the time, Pallas kernels for 1%

profile of v8, /device:TPU:1, one launch (start us, length us, event | category | flops | bytes accessed | tf_op | source)
XLA Modules:
  0.0 252.5 jit_solution(11736842441029055080)
XLA Ops:
  0.6 5.7 %collective-permute-start.1 = (bf16[256,1024]{1,0:T(8,128)(2,1)}, bf16[256,1024]{1,0:T(8,128)(2,1)S(1)}, u32[]{:S(2)}, u32[]{:S(2)}) collective-permute-start(bf16[256,1024]{1,0:T(8,128)(2,1)} %refs_0_.3), channel_id=1, source_target_pairs={{64,0},{96,32},{0,64},{32,96},{65,1},{97,33},{1,65},{33,97},{66,2}... | collective-permute-start | bytes 1572872 | tf_op jit(solution)/shard_map/ppermute | solution.py:265
  6.3 2.7 %collective-permute-start = (bf16[256,1024]{1,0:T(8,128)(2,1)}, bf16[256,1024]{1,0:T(8,128)(2,1)S(1)}, u32[]{:S(2)}, u32[]{:S(2)}) collective-permute-start(bf16[256,1024]{1,0:T(8,128)(2,1)} %refs_0_.3), channel_id=1, source_target_pairs={{32,0},{64,32},{96,64},{0,96},{33,1},{65,33},{97,65},{1,97},{34,2}... | collective-permute-start | bytes 1572872 | tf_op jit(solution)/shard_map/ppermute | solution.py:265
  9.0 2.6 %collective-permute-start.2 = (bf16[256,1024]{1,0:T(8,128)(2,1)}, bf16[256,1024]{1,0:T(8,128)(2,1)S(1)}, u32[]{:S(2)}, u32[]{:S(2)}) collective-permute-start(bf16[256,1024]{1,0:T(8,128)(2,1)} %refs_0_.3), channel_id=1, source_target_pairs={{96,0},{0,32},{32,64},{64,96},{97,1},{1,33},{33,65},{65,97},{98,2}... | collective-permute-start | bytes 1572872 | tf_op jit(solution)/shard_map/ppermute | solution.py:265
  12.3 0.9 copy-done.3
  13.2 0.8 copy-done.4
  14.0 0.8 copy-done.5
  14.7 1.3 shard_map.95
  16.0 26.9 %all_to_all.65 = bf16[4,16,1024]{2,1,0:T(8,128)(2,1)S(1)} all-to-all(bf16[4,16,1024]{2,1,0:T(8,128)(2,1)S(1)} %get-tuple-element.23), channel_id=1, replica_groups=mesh['zh'=4,'y'=4,'x'=4,'zl'=4,'c'=2] {'zh'}, dimensions={0} | all-to-all | bytes 262144 | tf_op jit(solution)/shard_map/all_to_all | solution.py:239
  43.0 10.1 %all_to_all.66 = bf16[4,4,16,1024]{3,2,1,0:T(8,128)(2,1)S(1)} all-to-all(bf16[4,4,16,1024]{3,2,1,0:T(8,128)(2,1)S(1)} %broadcast_in_dim.2), channel_id=1, replica_groups=mesh['zh'=4,'y'=4,'x'=4,'zl'=4,'c'=2] {'y'}, dimensions={0} | all-to-all | bytes 1048576 | tf_op jit(solution)/shard_map/all_to_all | solution.py:239
  53.2 0.5 shard_map.96
  53.7 8.0 %all_to_all.67.lin_ref = bf16[4,4,2,16,256]{4,3,2,1,0:T(8,128)(2,1)S(1)} all-to-all(bf16[4,4,2,16,256]{4,3,2,1,0:T(8,128)(2,1)S(1)} %get-tuple-element.25), channel_id=1, replica_groups=mesh['zh'=4,'y'=4,'x'=4,'zl'=4,'c'=2] {'y'}, dimensions={0} | all-to-all | bytes 524288 | tf_op jit(solution)/shard_map/all_to_all | solution.py:239
  61.7 0.5 shard_map.97
  62.2 18.3 %all_to_all.68.blocks_ref = bf16[4,2,16,1024]{3,2,1,0:T(8,128)(2,1)S(1)} all-to-all(bf16[4,2,16,1024]{3,2,1,0:T(8,128)(2,1)S(1)} %bitcast.19), channel_id=1, replica_groups=mesh['zh'=4,'y'=4,'x'=4,'zl'=4,'c'=2] {'zh'}, dimensions={0} | all-to-all | bytes 524288 | tf_op jit(solution)/shard_map/all_to_all | solution.py:239
  80.6 18.4 %all_to_all.69 = bf16[4,2,16,1024]{3,2,1,0:T(8,128)(2,1)S(1)} all-to-all(bf16[4,2,16,1024]{3,2,1,0:T(8,128)(2,1)S(1)} %shard_map.98), channel_id=1, replica_groups=mesh['zh'=4,'y'=4,'x'=4,'zl'=4,'c'=2] {'zh'}, dimensions={0} | all-to-all | bytes 524288 | tf_op jit(solution)/shard_map/all_to_all | solution.py:239
  99.0 0.8 shard_map.99
  99.8 7.9 %all_to_all.70 = bf16[4,128,256]{2,1,0:T(8,128)(2,1)S(1)} all-to-all(bf16[4,128,256]{2,1,0:T(8,128)(2,1)S(1)} %shard_map.99), channel_id=1, replica_groups=mesh['zh'=4,'y'=4,'x'=4,'zl'=4,'c'=2] {'y'}, dimensions={0} | all-to-all | bytes 524288 | tf_op jit(solution)/shard_map/all_to_all | solution.py:239
  108.2 12.0 %all-gather = bf16[1024,256]{1,0:T(8,128)(2,1)S(1)} all-gather(bf16[512,256]{1,0:T(8,128)(2,1)S(1)} %get-tuple-element.35), channel_id=2, replica_groups=mesh['zh'=4,'y'=4,'x'=4,'zl'=4,'c'=2] {'c'}, dimensions={0}, use_global_device_ids=true | all-gather | bytes 786432 | tf_op jit(solution)/shard_map/all_gather | solution.py:248
  120.3 15.2 %all_to_all.71.blocks_ref = bf16[16,32,256]{2,1,0:T(8,128)(2,1)S(1)} all-to-all(bf16[16,32,256]{2,1,0:T(8,128)(2,1)S(1)} %bitcast.22), channel_id=1, replica_groups=mesh['zh'=4,'y'=4,'x'=4,'zl'=4,'c'=2] {'x','zl'}, dimensions={0} | all-to-all | bytes 524288 | tf_op jit(solution)/shard_map/all_to_all | solution.py:239
  135.5 13.1 %all_to_all.72 = bf16[16,32,256]{2,1,0:T(8,128)(2,1)S(1)} all-to-all(bf16[16,32,256]{2,1,0:T(8,128)(2,1)S(1)} %shard_map.102), channel_id=1, replica_groups=mesh['zh'=4,'y'=4,'x'=4,'zl'=4,'c'=2] {'x','zl'}, dimensions={0} | all-to-all | bytes 524288 | tf_op jit(solution)/shard_map/all_to_all | solution.py:239
  148.6 4.0 %all_gather.26.first_ref = bf16[1024,256]{1,0:T(8,128)(2,1)S(1)} all-gather(bf16[512,256]{1,0:T(8,128)(2,1)S(1)} %bitcast.24), channel_id=1, replica_groups=mesh['zh'=4,'y'=4,'x'=4,'zl'=4,'c'=2] {'c'}, dimensions={0}, use_global_device_ids=true | all-gather | bytes 786432 | tf_op jit(solution)/shard_map/all_gather | solution.py:253
  153.0 7.2 %all_to_all.73.lin_ref = bf16[4,64,256]{2,1,0:T(8,128)(2,1)S(1)} all-to-all(bf16[4,64,256]{2,1,0:T(8,128)(2,1)S(1)} %get-tuple-element.36), channel_id=1, replica_groups=mesh['zh'=4,'y'=4,'x'=4,'zl'=4,'c'=2] {'y'}, dimensions={0} | all-to-all | bytes 262144 | tf_op jit(solution)/shard_map/all_to_all | solution.py:239
  160.2 0.5 shard_map.104
  160.7 26.6 %all-gather.1 = bf16[256,1024]{1,0:T(8,128)(2,1)S(1)} all-gather(bf16[64,1024]{1,0:T(8,128)(2,1)S(1)} %shard_map.104), channel_id=3, replica_groups=mesh['zh'=4,'y'=4,'x'=4,'zl'=4,'c'=2] {'zh'}, dimensions={0}, use_global_device_ids=true | all-gather | bytes 655360 | tf_op jit(solution)/shard_map/all_gather | solution.py:299
  187.3 0.8 shard_map.105
  188.1 7.2 %all_to_all.74.moved_ref = bf16[4,64,256]{2,1,0:T(8,128)(2,1)S(1)} all-to-all(bf16[4,64,256]{2,1,0:T(8,128)(2,1)S(1)} %shard_map.105), channel_id=1, replica_groups=mesh['zh'=4,'y'=4,'x'=4,'zl'=4,'c'=2] {'y'}, dimensions={0} | all-to-all | bytes 262144 | tf_op jit(solution)/shard_map/all_to_all | solution.py:239
  195.7 4.0 %all-gather.2 = bf16[1024,256]{1,0:T(8,128)(2,1)S(1)} all-gather(bf16[512,256]{1,0:T(8,128)(2,1)S(1)} %get-tuple-element.40), channel_id=4, replica_groups=mesh['zh'=4,'y'=4,'x'=4,'zl'=4,'c'=2] {'c'}, dimensions={0}, use_global_device_ids=true | all-gather | bytes 786432 | tf_op jit(solution)/shard_map/all_gather | solution.py:248
  199.8 12.6 %all_to_all.75.blocks_ref = bf16[16,32,256]{2,1,0:T(8,128)(2,1)S(1)} all-to-all(bf16[16,32,256]{2,1,0:T(8,128)(2,1)S(1)} %bitcast.23), channel_id=1, replica_groups=mesh['zh'=4,'y'=4,'x'=4,'zl'=4,'c'=2] {'x','zl'}, dimensions={0} | all-to-all | bytes 524288 | tf_op jit(solution)/shard_map/all_to_all | solution.py:239
  212.5 13.2 %all_to_all.76 = bf16[16,32,256]{2,1,0:T(8,128)(2,1)S(1)} all-to-all(bf16[16,32,256]{2,1,0:T(8,128)(2,1)S(1)} %shard_map.108), channel_id=1, replica_groups=mesh['zh'=4,'y'=4,'x'=4,'zl'=4,'c'=2] {'x','zl'}, dimensions={0} | all-to-all | bytes 524288 | tf_op jit(solution)/shard_map/all_to_all | solution.py:239
  225.7 4.0 %all_gather.31.second_ref = bf16[1024,256]{1,0:T(8,128)(2,1)S(1)} all-gather(bf16[512,256]{1,0:T(8,128)(2,1)S(1)} %bitcast.25), channel_id=1, replica_groups=mesh['zh'=4,'y'=4,'x'=4,'zl'=4,'c'=2] {'c'}, dimensions={0}, use_global_device_ids=true | all-gather | bytes 786432 | tf_op jit(solution)/shard_map/all_gather | solution.py:253
  229.6 1.7 shard_map.109
  231.3 20.5 %all_to_all.77.terms_ref = f32[16,1,128]{2,1,0:T(1,128)S(1)} all-to-all(f32[16,1,128]{2,1,0:T(1,128)S(1)} %get-tuple-element.43), channel_id=1, replica_groups=mesh['zh'=4,'y'=4,'x'=4,'zl'=4,'c'=2] {'y','zh'}, dimensions={0} | all-to-all | bytes 16384 | tf_op jit(solution)/shard_map/all_to_all | solution.py:239
  251.8 0.7 shard_map.110
  (23 shorter events, 1.5 us)
Async XLA Ops:
  0.6 11.6 %copy-start.6 = (s32[16]{0:T(128)S(1)}, s32[16]{0:T(128)}, u32[]{:S(2)}) copy-start(s32[16]{0:T(128)} %mask_ref.1) | copy-start | bytes 196
  0.6 42.3 %collective-permute-start.1 = (bf16[256,1024]{1,0:T(8,128)(2,1)}, bf16[256,1024]{1,0:T(8,128)(2,1)S(1)}, u32[]{:S(2)}, u32[]{:S(2)}) collective-permute-start(bf16[256,1024]{1,0:T(8,128)(2,1)} %refs_0_.3), channel_id=1, source_target_pairs={{64,0},{96,32},{0,64},{32,96},{65,1},{97,33},{1,65},{33,97},{66,2}... | collective-permute-start | bytes 1572872 | tf_op jit(solution)/shard_map/ppermute | solution.py:265
  6.3 36.7 %collective-permute-start = (bf16[256,1024]{1,0:T(8,128)(2,1)}, bf16[256,1024]{1,0:T(8,128)(2,1)S(1)}, u32[]{:S(2)}, u32[]{:S(2)}) collective-permute-start(bf16[256,1024]{1,0:T(8,128)(2,1)} %refs_0_.3), channel_id=1, source_target_pairs={{32,0},{64,32},{96,64},{0,96},{33,1},{65,33},{97,65},{1,97},{34,2}... | collective-permute-start | bytes 1572872 | tf_op jit(solution)/shard_map/ppermute | solution.py:265
  9.0 34.0 %collective-permute-start.2 = (bf16[256,1024]{1,0:T(8,128)(2,1)}, bf16[256,1024]{1,0:T(8,128)(2,1)S(1)}, u32[]{:S(2)}, u32[]{:S(2)}) collective-permute-start(bf16[256,1024]{1,0:T(8,128)(2,1)} %refs_0_.3), channel_id=1, source_target_pairs={{96,0},{0,32},{32,64},{64,96},{97,1},{1,33},{33,65},{65,97},{98,2}... | collective-permute-start | bytes 1572872 | tf_op jit(solution)/shard_map/ppermute | solution.py:265
  12.3 1.0 copy-start.3
  13.2 0.8 copy-start.4
  14.0 0.8 copy-start.5
  16.0 37.2 %copy-start.1 = (f32[1024,256]{1,0:T(8,128)S(1)}, f32[1024,256]{1,0:T(8,128)}, u32[]{:S(2)}) copy-start(f32[1024,256]{1,0:T(8,128)} %query_ref.3) | copy-start | bytes 3145732
  43.0 10.1 %copy-start.2 = (bf16[1024,256]{1,0:T(8,128)(2,1)S(1)}, bf16[1024,256]{1,0:T(8,128)(2,1)}, u32[]{:S(2)}) copy-start(bf16[1024,256]{1,0:T(8,128)(2,1)} %up_ref.1) | copy-start | bytes 1572868
  53.7 8.1 %copy-start = (bf16[256,1024]{1,0:T(8,128)(2,1)S(1)}, bf16[256,1024]{1,0:T(8,128)(2,1)}, u32[]{:S(2)}) copy-start(bf16[256,1024]{1,0:T(8,128)(2,1)} %refs_0_.3) | copy-start | bytes 1572868
